TPU v7x, 512 devices: a whole 4x4x16 slice. The times are simulated.
512 devices in a mesh: node: 16 (over z), tm: 32 (over y, x, core).
Axes of the slice: x: 4, y: 4, z: 16, core: 2. Of those that a mesh axis runs over, the one named last changes fastest.
Arguments:
- series: bfloat16 [4096, 16384], P('node', 'tm'), may hold values from -6 to 6
- conv_weight: bfloat16 [128, 128], replicated, may hold values from -0.5 to 0.5
- conv_bias: float32 [128], replicated, may hold values from -3 to 3
- mix_weight: bfloat16 [128, 64], replicated, may hold values from -0.75 to 0.75
- local_blocks: int32 [32, 2], P('node'), may hold values from 0 to 1
- local_values: bfloat16 [32, 2, 128, 128], P('node'), may hold values from -0.375 to 0.375
- send_rows: int32 [16, 16, 16], P('node'), may hold values from 0 to 255
- send_count: int32 [16, 16], replicated, may hold values from 0 to 16, as said below
- remote_values: bfloat16 [4096, 256], P('node'), may hold values from -1.5 to 1.5
- cotangent: bfloat16 [4096, 16384], P('node', 'tm'), may hold values from -6 to 6
Outputs:
- mixed_out: bfloat16 [4096, 16384], P('node', 'tm')
- input_grad: bfloat16 [4096, 16384], P('node', 'tm')
Inputs may be any that keep to these rules, and one draw needn't show every extreme that they name: `local_blocks`: tile index within the same group. `send_rows`: row index within the sending group. `send_count`: in every draw some group receives 16 live slots from every group.
All inputs are finite; a program needn't handle non-finite values.
Results may differ from a plain program's by a relative error of at most 0.009.
Values may be sent and summed in bfloat16 or wider, within the bound.
No kernel may reach another device: no remote copies, remote signals or barrier semaphores. Data moves between devices by JAX's collectives and lax.ppermute only.
A program may use at most 64 MiB of HBM per device.

v0:
```python
import jax
import jax.numpy as jnp
from jax import lax
from jax.sharding import PartitionSpec as P


def gated_preact(rows_now, rows_before, conv_weight, conv_bias):
    stacked = jnp.concatenate([rows_before, rows_now], axis=1)
    return jnp.dot(stacked, conv_weight, preferred_element_type=jnp.float32) + conv_bias


def activate(preact, width):
    filtered = jnp.tanh(preact[:, :width])
    opened = jax.nn.sigmoid(preact[:, width:])
    return (filtered * opened).astype(jnp.bfloat16)


def gate_grad(upstream, preact, width):
    upstream = lax.optimization_barrier(upstream).astype(jnp.float32)
    filtered = jnp.tanh(preact[:, :width])
    opened = jax.nn.sigmoid(preact[:, width:])
    first_half = upstream * opened * (1.0 - filtered * filtered)
    second_half = upstream * filtered * opened * (1.0 - opened)
    return jnp.concatenate([first_half, second_half], axis=1).astype(jnp.bfloat16)


def lagged_steps(current_block, shift_len):
    zeros = jnp.zeros(
        (current_block.shape[0], shift_len, current_block.shape[2]), current_block.dtype
    )
    return jnp.concatenate([zeros, current_block[:, : current_block.shape[1] - shift_len]], axis=1)


def forward_shift_steps(current_block, shift_len):
    zeros = jnp.zeros(
        (current_block.shape[0], shift_len, current_block.shape[2]), current_block.dtype
    )
    return jnp.concatenate([current_block[:, shift_len:], zeros], axis=1)


def local(
    series,
    conv_weight,
    conv_bias,
    mix_weight,
    local_blocks,
    local_values,
    send_rows,
    send_count,
    remote_values,
    cotangent,
):
    node_dev, columns = series.shape
    channels = mix_weight.shape[1]
    tile_count = local_blocks.shape[0]
    tile_size = local_values.shape[2]
    slot_cap = send_rows.shape[2]
    my_group = lax.axis_index("node")
    counts_in = lax.dynamic_slice_in_dim(send_count, my_group, 1, 1)[:, 0]
    alive = (jnp.arange(slot_cap, dtype=jnp.int32)[None, :] < counts_in[:, None]).reshape(-1)
    remote_live = remote_values * alive.astype(jnp.bfloat16)[None, :]
    node_rows = lax.all_to_all(series, "tm", split_axis=0, concat_axis=1, tiled=True)
    few_nodes = node_rows.shape[0]
    full_steps = node_rows.shape[1] // channels
    shift_len = full_steps // 2
    steps_block = node_rows.reshape(few_nodes, full_steps, channels)
    preact = gated_preact(
        steps_block.reshape(-1, channels),
        lagged_steps(steps_block, shift_len).reshape(-1, channels),
        conv_weight,
        conv_bias,
    )
    hidden_nodes = activate(preact, channels).reshape(few_nodes, full_steps * channels)
    hidden = lax.all_to_all(hidden_nodes, "tm", split_axis=1, concat_axis=0, tiled=True)
    hidden_tiles = hidden.reshape(tile_count, tile_size, columns)
    sources = jnp.take(hidden_tiles, local_blocks, axis=0)
    local_sum = jnp.einsum(
        "tbij,tbjc->tic", local_values, sources, preferred_element_type=jnp.float32
    ).reshape(node_dev, columns)
    own_rows = send_rows.reshape(-1)
    outgoing = jnp.take(hidden, own_rows, axis=0)
    remote_sum = jnp.dot(
        remote_live,
        lax.all_to_all(outgoing, "node", split_axis=0, concat_axis=0, tiled=True),
        preferred_element_type=jnp.float32,
    )
    mixed = (local_sum + remote_sum).astype(jnp.bfloat16)
    both = jnp.concatenate([hidden.reshape(-1, channels), mixed.reshape(-1, channels)], axis=1)
    projected = jnp.dot(both, mix_weight, preferred_element_type=jnp.float32)
    mixed_out = (
        (series.reshape(-1, channels).astype(jnp.float32) + projected)
        .astype(jnp.bfloat16)
        .reshape(node_dev, columns)
    )
    grads = jnp.dot(
        cotangent.reshape(-1, channels), mix_weight.T, preferred_element_type=jnp.float32
    )
    mixed_grad = grads[:, channels:].astype(jnp.bfloat16).reshape(node_dev, columns)
    slot_grads = jnp.dot(remote_live.T, mixed_grad, preferred_element_type=jnp.float32).astype(
        jnp.bfloat16
    )
    back_rows = lax.all_to_all(slot_grads, "node", split_axis=0, concat_axis=0, tiled=True)
    picker = (jnp.arange(node_dev, dtype=jnp.int32)[:, None] == own_rows[None, :]).astype(
        jnp.bfloat16
    )
    remote_grad = jnp.dot(picker, back_rows, preferred_element_type=jnp.float32)
    tiled_grad = mixed_grad.reshape(tile_count, tile_size, columns)
    contrib = jnp.einsum(
        "tbij,tic->tbjc", local_values, tiled_grad, preferred_element_type=jnp.float32
    )
    selector = (
        local_blocks[None, :, :] == jnp.arange(tile_count, dtype=jnp.int32)[:, None, None]
    ).astype(jnp.float32)
    local_grad = jnp.einsum("ktb,tbjc->kjc", selector, contrib).reshape(node_dev, columns)
    hidden_grad = (
        grads[:, :channels].reshape(node_dev, columns) + local_grad + remote_grad
    ).astype(jnp.bfloat16)
    grad_nodes = lax.all_to_all(hidden_grad, "tm", split_axis=0, concat_axis=1, tiled=True)
    gate_out = gate_grad(grad_nodes.reshape(-1, channels), preact, channels)
    conv_back = jnp.dot(gate_out, conv_weight.T, preferred_element_type=jnp.float32)
    previous_gradient = lax.optimization_barrier(
        conv_back[:, :channels].astype(jnp.bfloat16)
    ).reshape(few_nodes, full_steps, channels)
    future_values = forward_shift_steps(previous_gradient, shift_len)
    grad_local = (
        conv_back[:, channels:].reshape(few_nodes, full_steps, channels)
        + future_values.astype(jnp.float32)
    ).astype(jnp.bfloat16)
    conv_grad = lax.all_to_all(
        grad_local.reshape(few_nodes, full_steps * channels),
        "tm",
        split_axis=1,
        concat_axis=0,
        tiled=True,
    )
    conv_grad = lax.optimization_barrier(conv_grad)
    input_grad = (cotangent.astype(jnp.float32) + conv_grad.astype(jnp.float32)).astype(
        jnp.bfloat16
    )
    return (mixed_out, input_grad)


def solution(mesh):
    in_specs = (
        P("node", "tm"),
        P(),
        P(),
        P(),
        P("node", None),
        P("node", None, None, None),
        P("node", None, None),
        P(),
        P("node", None),
        P("node", "tm"),
    )
    out_specs = (P("node", "tm"), P("node", "tm"))
    return jax.shard_map(local, mesh=mesh, in_specs=in_specs, out_specs=out_specs, check_vma=False)
```

profile of v0, /device:TPU:32, one launch (start us, length us, event | category | flops | bytes accessed | tf_op | source)
XLA Modules:
  0.0 123.8 jit_solution(12358383753426694319)
XLA Ops:
  0.7 0.7 copy-done.7
  1.7 1.3 %reshape.154 = bf16[2048,64]{1,0:T(8,128)(2,1)S(1)} reshape(bf16[256,512]{1,0:T(8,128)(2,1)} %param.19) | data formatting | bytes 524288 | tf_op jit(solution)/shard_map/reshape | solution.py:96
  4.0 0.6 copy-done.3
  4.6 1.0 convolution_convert_fusion
  5.6 15.2 %all-to-all-start.3 = ((bf16[16,16,512]{2,1,0:T(8,128)(2,1)}), bf16[16,16,512]{2,1,0:T(8,128)(2,1)S(1)}, u32[]{:S(2)}, u32[]{:S(2)}) async-start(bf16[16,16,512]{2,1,0:T(8,128)(2,1)} %bitcast.21), calls=%async_computation.3 | async-start | bytes 524288 | tf_op jit(solution)/shard_map/all_to_all | solution.py:102
  21.5 0.5 copy.57
  22.3 0.9 convolution_bitcast_fusion.1
  23.3 0.9 slice-done
  24.9 13.8 %all-to-all-done.3 = bf16[16,16,512]{2,1,0:T(8,128)(2,1)S(1)} async-done(((bf16[16,16,512]{2,1,0:T(8,128)(2,1)}), bf16[16,16,512]{2,1,0:T(8,128)(2,1)S(1)}, u32[]{:S(2)}, u32[]{:S(2)}) %all-to-all-start.3) | async-done | bytes 262176 | tf_op jit(solution)/shard_map/all_to_all | solution.py:102
  38.7 7.4 %all-to-all-start = ((bf16[32,8,512]{2,1,0:T(8,128)(2,1)}), bf16[32,8,512]{2,1,0:T(8,128)(2,1)S(1)}, u32[]{:S(2)}, u32[]{:S(2)}) async-start(bf16[32,8,512]{2,1,0:T(8,128)(2,1)} %bitcast), calls=%async_computation | async-start | bytes 524288 | tf_op jit(solution)/shard_map/all_to_all | solution.py:62
  46.4 1.0 fusion.3
  47.3 7.8 %all-to-all-done = bf16[32,8,512]{2,1,0:T(8,128)(2,1)S(1)} async-done(((bf16[32,8,512]{2,1,0:T(8,128)(2,1)}), bf16[32,8,512]{2,1,0:T(8,128)(2,1)S(1)}, u32[]{:S(2)}, u32[]{:S(2)}) %all-to-all-start) | async-done | bytes 262176 | tf_op jit(solution)/shard_map/all_to_all | solution.py:62
  55.1 3.9 %all-to-all-start.4 = ((bf16[32,8,512]{2,1,0:T(8,128)(2,1)}), bf16[32,8,512]{2,1,0:T(8,128)(2,1)S(1)}, u32[]{:S(2)}, u32[]{:S(2)}) async-start(bf16[32,8,512]{2,1,0:T(8,128)(2,1)} %fusion.3), calls=%async_computation.4 | async-start | bytes 524288 | tf_op jit(solution)/shard_map/all_to_all | solution.py:118
  59.8 0.6 copy-done.4
  60.4 0.5 convolution_add_fusion
  60.9 7.0 %all-to-all-done.4 = bf16[32,8,512]{2,1,0:T(8,128)(2,1)S(1)} async-done(((bf16[32,8,512]{2,1,0:T(8,128)(2,1)}), bf16[32,8,512]{2,1,0:T(8,128)(2,1)S(1)}, u32[]{:S(2)}, u32[]{:S(2)}) %all-to-all-start.4) | async-done | bytes 262176 | tf_op jit(solution)/shard_map/all_to_all | solution.py:118
  70.4 0.9 copy.50
  71.2 3.9 %all-to-all-start.1 = ((bf16[8,32,512]{2,0,1:T(8,128)(2,1)}), bf16[8,32,512]{2,0,1:T(8,128)(2,1)S(1)}, u32[]{:S(2)}, u32[]{:S(2)}) async-start(bf16[8,32,512]{2,0,1:T(8,128)(2,1)} %copy.50), calls=%async_computation.1 | async-start | bytes 524288 | tf_op jit(solution)/shard_map/all_to_all | solution.py:74
  75.6 0.8 copy.64
  76.4 7.6 %all-to-all-done.1 = bf16[8,32,512]{2,0,1:T(8,128)(2,1)S(1)} async-done(((bf16[8,32,512]{2,0,1:T(8,128)(2,1)}), bf16[8,32,512]{2,0,1:T(8,128)(2,1)S(1)}, u32[]{:S(2)}, u32[]{:S(2)}) %all-to-all-start.1) | async-done | bytes 262176 | tf_op jit(solution)/shard_map/all_to_all | solution.py:74
  84.0 3.9 %all-to-all-start.5 = ((bf16[8,32,512]{2,0,1:T(8,128)(2,1)}), bf16[8,32,512]{2,0,1:T(8,128)(2,1)S(1)}, u32[]{:S(2)}, u32[]{:S(2)}) async-start(bf16[8,32,512]{2,0,1:T(8,128)(2,1)} %copy.64), calls=%async_computation.5 | async-start | bytes 524288 | tf_op jit(solution)/shard_map/all_to_all | solution.py:129
  87.9 1.2 reshape.162
  89.1 1.2 gather_fusion.1
  90.2 0.8 broadcast_select_fusion
  91.0 5.8 %all-to-all-done.5 = bf16[8,32,512]{2,0,1:T(8,128)(2,1)S(1)} async-done(((bf16[8,32,512]{2,0,1:T(8,128)(2,1)}), bf16[8,32,512]{2,0,1:T(8,128)(2,1)S(1)}, u32[]{:S(2)}, u32[]{:S(2)}) %all-to-all-start.5) | async-done | bytes 262176 | tf_op jit(solution)/shard_map/all_to_all | solution.py:129
  96.8 6.3 %all-to-all-start.2 = ((bf16[16,16,512]{2,1,0:T(8,128)(2,1)}), bf16[16,16,512]{2,1,0:T(8,128)(2,1)S(1)}, u32[]{:S(2)}, u32[]{:S(2)}) async-start(bf16[16,16,512]{2,1,0:T(8,128)(2,1)} %broadcast_select_fusion), calls=%async_computation.2 | async-start | bytes 524288 | tf_op jit(solution)/shard_map/all_to_all | solution.py:84
  103.8 0.6 gather_fusion
  104.4 0.4 copy-done.2
  104.7 0.8 add_convert_fusion.1
  105.8 15.7 %all-to-all-done.2 = bf16[16,16,512]{2,1,0:T(8,128)(2,1)S(1)} async-done(((bf16[16,16,512]{2,1,0:T(8,128)(2,1)}), bf16[16,16,512]{2,1,0:T(8,128)(2,1)S(1)}, u32[]{:S(2)}, u32[]{:S(2)}) %all-to-all-start.2) | async-done | bytes 262176 | tf_op jit(solution)/shard_map/all_to_all | solution.py:84
  122.0 0.5 fusion
  122.8 1.0 reshape.153
  (65 shorter events, 8.6 us)
Async XLA Ops:
  0.6 20.5 %copy-start = (bf16[2,2,128,128]{3,2,1,0:T(8,128)(2,1)S(1)}, bf16[2,2,128,128]{3,2,1,0:T(8,128)(2,1)}, u32[]{:S(2)}) copy-start(bf16[2,2,128,128]{3,2,1,0:T(8,128)(2,1)} %param.15) | copy-start | bytes 393220
  0.6 0.7 copy-start.7
  1.7 1.3 %copy-start.6 = (bf16[128,64]{0,1:T(8,128)(2,1)S(1)}, bf16[128,64]{0,1:T(8,128)(2,1)}, u32[]{:S(2)}) copy-start(bf16[128,64]{0,1:T(8,128)(2,1)} %param.13) | copy-start | bytes 49156
  3.4 17.8 %copy-start.1 = (f32[2048,128]{0,1:T(8,128)}, f32[2048,128]{0,1:T(8,128)S(1)}, u32[]{:S(2)}) copy-start(f32[2048,128]{0,1:T(8,128)S(1)} %fusion.41) | copy-start | bytes 3145732
  3.7 0.9 copy-start.3
  5.6 33.1 %all-to-all-start.3 = ((bf16[16,16,512]{2,1,0:T(8,128)(2,1)}), bf16[16,16,512]{2,1,0:T(8,128)(2,1)S(1)}, u32[]{:S(2)}, u32[]{:S(2)}) async-start(bf16[16,16,512]{2,1,0:T(8,128)(2,1)} %bitcast.21), calls=%async_computation.3 | async-start | bytes 524288 | tf_op jit(solution)/shard_map/all_to_all | solution.py:102
  21.5 0.7 copy-start.8
  23.2 1.0 slice-start
  38.7 7.5 %copy-start.5 = (s32[1,16,16]{2,1,0:T(8,128)S(1)}, s32[1,16,16]{2,1,0:T(8,128)}, u32[]{:S(2)}) copy-start(s32[1,16,16]{2,1,0:T(8,128)} %param.16) | copy-start | bytes 3076
  38.7 16.4 %all-to-all-start = ((bf16[32,8,512]{2,1,0:T(8,128)(2,1)}), bf16[32,8,512]{2,1,0:T(8,128)(2,1)S(1)}, u32[]{:S(2)}, u32[]{:S(2)}) async-start(bf16[32,8,512]{2,1,0:T(8,128)(2,1)} %bitcast), calls=%async_computation | async-start | bytes 524288 | tf_op jit(solution)/shard_map/all_to_all | solution.py:62
  55.1 12.8 %all-to-all-start.4 = ((bf16[32,8,512]{2,1,0:T(8,128)(2,1)}), bf16[32,8,512]{2,1,0:T(8,128)(2,1)S(1)}, u32[]{:S(2)}, u32[]{:S(2)}) async-start(bf16[32,8,512]{2,1,0:T(8,128)(2,1)} %fusion.3), calls=%async_computation.4 | async-start | bytes 524288 | tf_op jit(solution)/shard_map/all_to_all | solution.py:118
  59.6 0.8 copy-start.4
  59.7 0.7 copy-start.9
  71.2 12.8 %all-to-all-start.1 = ((bf16[8,32,512]{2,0,1:T(8,128)(2,1)}), bf16[8,32,512]{2,0,1:T(8,128)(2,1)S(1)}, u32[]{:S(2)}, u32[]{:S(2)}) async-start(bf16[8,32,512]{2,0,1:T(8,128)(2,1)} %copy.50), calls=%async_computation.1 | async-start | bytes 524288 | tf_op jit(solution)/shard_map/all_to_all | solution.py:74
  84.0 12.8 %all-to-all-start.5 = ((bf16[8,32,512]{2,0,1:T(8,128)(2,1)}), bf16[8,32,512]{2,0,1:T(8,128)(2,1)S(1)}, u32[]{:S(2)}, u32[]{:S(2)}) async-start(bf16[8,32,512]{2,0,1:T(8,128)(2,1)} %copy.64), calls=%async_computation.5 | async-start | bytes 524288 | tf_op jit(solution)/shard_map/all_to_all | solution.py:129
  96.8 24.7 %all-to-all-start.2 = ((bf16[16,16,512]{2,1,0:T(8,128)(2,1)}), bf16[16,16,512]{2,1,0:T(8,128)(2,1)S(1)}, u32[]{:S(2)}, u32[]{:S(2)}) async-start(bf16[16,16,512]{2,1,0:T(8,128)(2,1)} %broadcast_select_fusion), calls=%async_computation.2 | async-start | bytes 524288 | tf_op jit(solution)/shard_map/all_to_all | solution.py:84
  103.8 1.0 copy-start.2
where the time goes:
time: 125 us; the launch traced here: 124 us
  waiting for transfers between devices  57.6 us (46%)
  starting transfers between devices  40.5 us (32%)
  local copies, waits for them, and re-layouts  17.2 us (14%)
  matrix products  5.25 us (4%)
  other arithmetic  2.21 us (2%)
    all_to_all x1, waiting for transfers between devices, local(): lax.all_to_all(outgoing, 'node', split_axis=0, concat_axis=0, tiled=True)  15.7 us
    all_to_all x1, starting transfers between devices, local(): lax.all_to_all(slot_grads, 'node', split_axis=0, concat_axis=0, tiled=True)  15.2 us
    all_to_all x1, waiting for transfers between devices, local(): lax.all_to_all(slot_grads, 'node', split_axis=0, concat_axis=0, tiled=True)  13.8 us
    all_to_all x1, waiting for transfers between devices, local(): lax.all_to_all(series, 'tm', split_axis=0, concat_axis=1, tiled=True)  7.76 us
    all_to_all x1, waiting for transfers between devices, local(): lax.all_to_all(hidden_nodes, 'tm', split_axis=1, concat_axis=0, tiled=True)  7.61 us
    all_to_all x1, starting transfers between devices, local(): lax.all_to_all(series, 'tm', split_axis=0, concat_axis=1, tiled=True)  7.44 us
    all_to_all x1, waiting for transfers between devices, local(): lax.all_to_all(hidden_grad, 'tm', split_axis=0, concat_axis=1, tiled=True)  6.96 us
    all_to_all x1, starting transfers between devices, local(): lax.all_to_all(outgoing, 'node', split_axis=0, concat_axis=0, tiled=True)  6.25 us
  transfers between devices with their start and end apart: 6, of which 6 were waited for; matrix products, arithmetic and copies ran while one was open for 9% of the time, Pallas kernels for 0%

commit v1 on v0

v1 whole, which is shorter than its diff:
```python
import jax
import jax.numpy as jnp
from jax import lax
from jax.experimental import pallas as pl
from jax.experimental.pallas import tpu as pltpu
from jax.sharding import PartitionSpec as P

C = 64
PAIR = 2 * C
F32 = jnp.float32
BF16 = jnp.bfloat16


def dot(a, b):
    return lax.dot_general(a, b, (((1,), (0,)), ((), ())), preferred_element_type=F32)


def dot_nt(a, b):
    return lax.dot_general(a, b, (((1,), (1,)), ((), ())), preferred_element_type=F32)


def dot_tn(a, b):
    return lax.dot_general(a, b, (((0,), (0,)), ((), ())), preferred_element_type=F32)


def low_lanes(shape):
    return lax.broadcasted_iota(jnp.int32, shape, 1) < C


def conv_pair(weight_ref):
    weight = weight_ref[...].astype(F32)
    turned = pltpu.roll(weight, C, 1)
    low = low_lanes(weight.shape)
    even = jnp.concatenate([jnp.where(low, weight, 0.0), jnp.where(low, turned, 0.0)], axis=1)
    odd = jnp.concatenate([jnp.where(low, 0.0, turned), jnp.where(low, 0.0, weight)], axis=1)
    return jnp.concatenate([even[:C], odd[:C], even[C:], odd[C:]], axis=0).astype(BF16)


def mix_pair(weight_ref):
    weight = weight_ref[...].astype(F32)
    twice = jnp.concatenate([weight, weight], axis=1)
    low = low_lanes(twice.shape)
    even, odd = jnp.where(low, twice, 0.0), jnp.where(low, 0.0, twice)
    return jnp.concatenate([even[:C], odd[:C], even[C:], odd[C:]], axis=0).astype(BF16)


def live_values(values_ref, count_ref):
    groups = count_ref.shape[0]
    slots = values_ref.shape[1]
    cap = slots // groups
    me = lax.axis_index("node")
    column = lax.broadcasted_iota(jnp.int32, (8, slots), 1)
    limit = jnp.zeros((8, slots), jnp.int32)
    for p in range(groups):
        limit = jnp.where(column >= p * cap, p * cap + count_ref[p, me], limit)
    alive = (column < limit)[:1]
    return jnp.where(alive, values_ref[...].astype(F32), 0.0).astype(BF16)


def picker(rows_ref, nodes):
    slots = rows_ref.shape[1]
    node = lax.broadcasted_iota(jnp.int32, (nodes, slots), 0)
    return jnp.where(node == rows_ref[...], 1.0, 0.0).astype(BF16)


def gates(series_ref, delayed_ref, weight, bias_ref, j):
    bias = bias_ref[...]
    turned = pltpu.roll(jnp.broadcast_to(bias, (8, PAIR)), C, 1)[:1]
    low = low_lanes(bias.shape)
    both = jnp.concatenate([jnp.where(low, bias, turned), jnp.where(low, turned, bias)], axis=1)
    cols = pl.ds(j * PAIR, PAIR)
    stacked = jnp.concatenate([delayed_ref[:, cols], series_ref[:, cols]], axis=1)
    preact = dot(stacked, weight) + both
    return jnp.tanh(preact[:, :PAIR]), jax.nn.sigmoid(preact[:, PAIR:])


def slot_grads_kernel(cot_ref, mix_ref, values_ref, count_ref, out_ref):
    mix = mix_pair(mix_ref)
    live = live_values(values_ref, count_ref)
    for j in range(cot_ref.shape[1] // PAIR):
        cols = pl.ds(j * PAIR, PAIR)
        mixed_grad = dot_nt(cot_ref[:, cols], mix[PAIR:]).astype(BF16)
        out_ref[:, cols] = dot_tn(live, mixed_grad).astype(BF16)


def hidden_kernel(series_ref, delayed_ref, conv_ref, bias_ref, rows_ref, hidden_ref, out_ref):
    weight = conv_pair(conv_ref)
    pick = picker(rows_ref, series_ref.shape[0])
    for j in range(series_ref.shape[1] // PAIR):
        cols = pl.ds(j * PAIR, PAIR)
        filtered, opened = gates(series_ref, delayed_ref, weight, bias_ref, j)
        hidden = (filtered * opened).astype(BF16)
        hidden_ref[:, cols] = hidden
        out_ref[:, cols] = dot_tn(pick, hidden).astype(BF16)


def local_grad_kernel(cot_ref, mix_ref, local_ref, blocks_ref, out_ref):
    mix = mix_pair(mix_ref)
    tiles, per_tile, size, _ = local_ref.shape
    kept = []
    for j in range(cot_ref.shape[1] // PAIR):
        cols = pl.ds(j * PAIR, PAIR)
        grads = dot_nt(cot_ref[:, cols], mix)
        out_ref[:, cols] = grads[:, :PAIR]
        kept.append(grads[:, PAIR:].astype(BF16))
    mixed_grad = jnp.concatenate(kept, axis=1)
    for t in range(tiles):
        for b in range(per_tile):
            rows = pl.ds(pl.multiple_of(blocks_ref[t, b] * size, size), size)
            out_ref[rows, :] += dot_tn(local_ref[t, b], mixed_grad[t * size : (t + 1) * size])


def mixed_kernel(
    series_ref, hidden_ref, slots_ref, mix_ref, local_ref, blocks_ref, values_ref, count_ref, out_ref
):
    mix = mix_pair(mix_ref)
    live = live_values(values_ref, count_ref)
    tiles, per_tile, size, _ = local_ref.shape
    remote = dot(live, slots_ref[...])
    sums = []
    for t in range(tiles):
        total = remote[t * size : (t + 1) * size]
        for b in range(per_tile):
            rows = pl.ds(pl.multiple_of(blocks_ref[t, b] * size, size), size)
            total += dot(local_ref[t, b], hidden_ref[rows, :])
        sums.append(total.astype(BF16))
    mixed = jnp.concatenate(sums, axis=0)
    for j in range(series_ref.shape[1] // PAIR):
        cols = pl.ds(j * PAIR, PAIR)
        both = jnp.concatenate([hidden_ref[:, cols], mixed[:, j * PAIR : (j + 1) * PAIR]], axis=1)
        out_ref[:, cols] = (series_ref[:, cols].astype(F32) + dot(both, mix)).astype(BF16)


def conv_grad_kernel(
    series_ref, delayed_ref, conv_ref, bias_ref, rows_ref, partial_ref, back_ref, before_ref, now_ref
):
    weight = conv_pair(conv_ref)
    pick = picker(rows_ref, series_ref.shape[0])
    for j in range(series_ref.shape[1] // PAIR):
        cols = pl.ds(j * PAIR, PAIR)
        upstream = partial_ref[:, cols] + dot(pick, back_ref[:, cols])
        upstream = upstream.astype(BF16).astype(F32)
        filtered, opened = gates(series_ref, delayed_ref, weight, bias_ref, j)
        first = upstream * opened * (1.0 - filtered * filtered)
        second = upstream * filtered * opened * (1.0 - opened)
        gate_grad = jnp.concatenate([first, second], axis=1).astype(BF16)
        back = dot_nt(gate_grad, weight)
        before_ref[:, cols] = back[:, :PAIR].astype(BF16)
        now_ref[:, cols] = back[:, PAIR:]


def input_grad_kernel(cot_ref, now_ref, later_ref, out_ref):
    grad = (now_ref[...] + later_ref[...].astype(F32)).astype(BF16)
    out_ref[...] = (cot_ref[...].astype(F32) + grad.astype(F32)).astype(BF16)


VMEM = pl.BlockSpec(memory_space=pltpu.VMEM)
SMEM = pl.BlockSpec(memory_space=pltpu.SMEM)


def call(kernel, specs, outs, flops, *args):
    many = isinstance(outs, tuple)
    return pl.pallas_call(
        kernel,
        out_shape=outs,
        in_specs=specs,
        out_specs=tuple(VMEM for _ in outs) if many else VMEM,
        compiler_params=pltpu.CompilerParams(vmem_limit_bytes=32 << 20),
        cost_estimate=pl.CostEstimate(flops=flops, bytes_accessed=1 << 20, transcendentals=0),
    )(*args)


def local(
    series,
    conv_weight,
    conv_bias,
    mix_weight,
    local_blocks,
    local_values,
    send_rows,
    send_count,
    remote_values,
    cotangent,
):
    nodes, columns = series.shape
    groups = send_rows.shape[1]
    cap = send_rows.shape[2]
    half = 16
    rows_bf = jax.ShapeDtypeStruct((nodes, columns), BF16)
    rows_f32 = jax.ShapeDtypeStruct((nodes, columns), F32)
    own_rows = send_rows.reshape(1, -1)
    bias = conv_bias.reshape(1, -1)

    def exchange(x):
        y = lax.all_to_all(x.reshape(groups, cap, columns), "node", 0, 0, tiled=True)
        return y.reshape(groups * cap, columns)

    delayed = lax.ppermute(series, "tm", [(i, i + half) for i in range(half)])
    slot_grads = call(
        slot_grads_kernel, [VMEM, VMEM, VMEM, SMEM], rows_bf, 100 << 20, cotangent, mix_weight, remote_values, send_count
    )
    back_rows = exchange(slot_grads)
    partial = call(
        local_grad_kernel, [VMEM, VMEM, VMEM, SMEM], rows_f32, 100 << 20, cotangent, mix_weight, local_values, local_blocks
    )
    hidden, outgoing = call(
        hidden_kernel,
        [VMEM] * 5,
        (rows_bf, rows_bf),
        100 << 20,
        series,
        delayed,
        conv_weight,
        bias,
        own_rows,
    )
    slots = exchange(outgoing)
    before, now = call(
        conv_grad_kernel,
        [VMEM] * 7,
        (rows_bf, rows_f32),
        100 << 20,
        series,
        delayed,
        conv_weight,
        bias,
        own_rows,
        partial,
        back_rows,
    )
    later = lax.ppermute(before, "tm", [(i + half, i) for i in range(half)])
    mixed_out = call(
        mixed_kernel,
        [VMEM] * 5 + [SMEM, VMEM, SMEM],
        rows_bf,
        100 << 20,
        series,
        hidden,
        slots,
        mix_weight,
        local_values,
        local_blocks,
        remote_values,
        send_count,
    )
    input_grad = call(input_grad_kernel, [VMEM] * 3, rows_bf, 1 << 20, cotangent, now, later)
    return (mixed_out, input_grad)


def solution(mesh):
    in_specs = (
        P("node", "tm"),
        P(),
        P(),
        P(),
        P("node", None),
        P("node", None, None, None),
        P("node", None, None),
        P(),
        P("node", None),
        P("node", "tm"),
    )
    out_specs = (P("node", "tm"), P("node", "tm"))
    return jax.shard_map(local, mesh=mesh, in_specs=in_specs, out_specs=out_specs, check_vma=False)
```

time: 125 us -> 66.9 us (0.54)
  the two profiles are of different devices: /device:TPU:32 before, /device:TPU:26 now
where the time goes in v1:
time: 66.9 us; the launch traced here: 66.4 us
  waiting for transfers between devices  28.6 us (43%)
  starting transfers between devices  25.7 us (38%)
  Pallas kernels  8.56 us (13%)
  local copies, waits for them, and re-layouts  2.8 us (4%)
  between operations  0.76 us (1%)
    all_to_all x2, starting transfers between devices, exchange(): lax.all_to_all(x.reshape(groups, cap, columns), 'node', 0, 0, tiled=True)  21.6 us
    all_to_all x2, waiting for transfers between devices, exchange(): lax.all_to_all(x.reshape(groups, cap, columns), 'node', 0, 0, tiled=True)  18.9 us
    ppermute x1, waiting for transfers between devices, local(): delayed = lax.ppermute(series, 'tm', [(i, i + half) for i in range(half)])  9.77 us
    pallas_call x6, Pallas kernels, call(): pl.pallas_call(kernel, out_shape=outs, in_specs=specs, out_specs=tuple((V...  8.56 us
    ppermute x1, starting transfers between devices, local(): later = lax.ppermute(before, 'tm', [(i + half, i) for i in range(half)])  2.8 us
    unnamed x23, local copies, waits for them, and re-layouts  2.72 us
  transfers between devices with their start and end apart: 4, of which 3 were waited for; matrix products, arithmetic and copies ran while one was open for 0% of the time, Pallas kernels for 9%

profile of v1, /device:TPU:26, one launch (start us, length us, event | category | flops | bytes accessed | tf_op | source)
XLA Modules:
  0.0 66.4 jit_solution(4224617711170953797)
XLA Ops:
  0.6 0.0 copy-start.7
  0.6 0.8 %copy.12.mix_ref = bf16[128,64]{1,0:T(8,128)(2,1)S(1)} copy(bf16[128,64]{0,1:T(8,128)(2,1)} %param.13) | data formatting | bytes 32768 | tf_op args[3]
  1.5 0.0 copy-done.7
  1.5 0.0 copy-start
  1.5 0.9 %copy-done = bf16[256,512]{1,0:T(8,128)(2,1)S(1)} copy-done((bf16[256,512]{1,0:T(8,128)(2,1)S(1)}, bf16[256,512]{1,0:T(8,128)(2,1)}, u32[]{:S(2)}) %copy-start) | copy-done | bytes 262168
  2.4 0.0 copy-start.4
  2.4 0.9 %copy-done.4 = bf16[256,256]{1,0:T(8,128)(2,1)S(1)} copy-done((bf16[256,256]{1,0:T(8,128)(2,1)S(1)}, bf16[256,256]{1,0:T(8,128)(2,1)}, u32[]{:S(2)}) %copy-start.4) | copy-done | bytes 131096
  3.3 2.1 %shard_map.116 = bf16[256,512]{1,0:T(8,128)(2,1)} custom-call(bf16[256,512]{1,0:T(8,128)(2,1)S(1)} %copy-done, bf16[128,64]{1,0:T(8,128)(2,1)S(1)} %copy.12.mix_ref, bf16[256,256]{1,0:T(8,128)(2,1)S(1)} %copy-done.4, s32[16,16]{1,0:T(8,128)S(1)} %copy-done.7), custom_call_target="tpu_custom_call" | custom-call | flops 104857600 | bytes 1048576 | tf_op jit(solution)/shard_map/pallas_call | solution.py:163
  5.4 0.0 copy-start.2
  5.4 15.3 %all-to-all-start.1 = ((bf16[16,16,512]{2,1,0:T(8,128)(2,1)}), bf16[16,16,512]{2,1,0:T(8,128)(2,1)S(1)}, u32[]{:S(2)}, u32[]{:S(2)}) async-start(bf16[16,16,512]{2,1,0:T(8,128)(2,1)} %bitcast.3), calls=%async_computation.1 | async-start | bytes 524288 | tf_op jit(solution)/shard_map/all_to_all | solution.py:195
  20.8 0.0 copy-done.2
  20.8 1.3 %collective-permute-start = (bf16[256,512]{1,0:T(8,128)(2,1)S(1)}, bf16[256,512]{1,0:T(8,128)(2,1)S(1)}, u32[]{:S(2)}, u32[]{:S(2)}) collective-permute-start(bf16[256,512]{1,0:T(8,128)(2,1)S(1)} %copy-done.2), channel_id=1, source_target_pairs={{0,16},{1,17},{2,18},{3,19},{4,20},{5,21},{6,22},{7,23},{8,24},{9,... | collective-permute-start | bytes 786440 | tf_op jit(solution)/shard_map/ppermute | solution.py:198
  22.1 0.0 copy-done.10
  22.1 0.1 reshape.23.rows_ref
  22.2 9.8 %collective-permute-done.delayed_ref = bf16[256,512]{1,0:T(8,128)(2,1)S(1)} collective-permute-done((bf16[256,512]{1,0:T(8,128)(2,1)S(1)}, bf16[256,512]{1,0:T(8,128)(2,1)S(1)}, u32[]{:S(2)}, u32[]{:S(2)}) %collective-permute-start) | collective-permute-done | bytes 262176 | tf_op jit(solution)/shard_map/ppermute | solution.py:198
  31.9 0.0 copy-done.6
  31.9 0.0 copy-done.9
  31.9 1.6 %shard_map.113 = (bf16[256,512]{1,0:T(8,128)(2,1)S(1)}, bf16[256,512]{1,0:T(8,128)(2,1)}) custom-call(bf16[256,512]{1,0:T(8,128)(2,1)S(1)} %copy-done.2, bf16[256,512]{1,0:T(8,128)(2,1)S(1)} %collective-permute-done.delayed_ref, bf16[128,128]{1,0:T(8,128)(2,1)S(1)} %copy-done.6, f32[1,128]{1,0:T(1,128)S(1)} %bitcast.7, s32[1,256]{1,0:T(1,128)S(1)} %reshape.23.rows_ref), custom_call_target="tpu_custom_call" | custom-call | flops 104857600 | bytes 1048576 | tf_op jit(solution)/shard_map/pallas_call | solution.py:163
  33.5 5.6 %all-to-all-done.1 = bf16[16,16,512]{2,1,0:T(8,128)(2,1)S(1)} async-done(((bf16[16,16,512]{2,1,0:T(8,128)(2,1)}), bf16[16,16,512]{2,1,0:T(8,128)(2,1)S(1)}, u32[]{:S(2)}, u32[]{:S(2)}) %all-to-all-start.1) | async-done | bytes 262176 | tf_op jit(solution)/shard_map/all_to_all | solution.py:195
  39.1 6.3 %all-to-all-start = ((bf16[16,16,512]{2,1,0:T(8,128)(2,1)}), bf16[16,16,512]{2,1,0:T(8,128)(2,1)S(1)}, u32[]{:S(2)}, u32[]{:S(2)}) async-start(bf16[16,16,512]{2,1,0:T(8,128)(2,1)} %bitcast.1), calls=%async_computation | async-start | bytes 524288 | tf_op jit(solution)/shard_map/all_to_all | solution.py:195
  45.4 0.0 copy-done.1
  45.4 0.0 copy-done.3
  45.4 0.0 copy-done.8
  45.5 1.1 %shard_map.115.partial_ref = f32[256,512]{1,0:T(8,128)S(1)} custom-call(bf16[256,512]{1,0:T(8,128)(2,1)S(1)} %copy-done.1, bf16[128,64]{1,0:T(8,128)(2,1)S(1)} %copy.12.mix_ref, bf16[2,2,128,128]{3,2,1,0:T(8,128)(2,1)S(1)} %copy-done.3, s32[2,2]{1,0:T(2,128)S(1)} %copy-done.8), custom_call_target="tpu_custom_call" | custom-call | flops 104857600 | bytes 1048576 | tf_op jit(solution)/shard_map/pallas_call | solution.py:163
  46.6 0.0 copy-start.5
  46.6 1.0 %shard_map.117 = (bf16[256,512]{1,0:T(8,128)(2,1)S(1)}, f32[256,512]{1,0:T(8,128)S(1)}) custom-call(bf16[256,512]{1,0:T(8,128)(2,1)S(1)} %copy-done.2, bf16[256,512]{1,0:T(8,128)(2,1)S(1)} %collective-permute-done.delayed_ref, bf16[128,128]{1,0:T(8,128)(2,1)S(1)} %copy-done.6, f32[1,128]{1,0:T(1,128)S(1)} %bitcast.8, s32[1,256]{1,0:T(1,128)S(1)} %reshape.23.rows_ref, ...), custom_call_target="tpu_custom_call" | custom-call | flops 104857600 | bytes 1048576 | tf_op jit(solution)/shard_map/pallas_call | solution.py:163
  47.6 2.8 %collective-permute-start.1 = (bf16[256,512]{1,0:T(8,128)(2,1)S(1)}, bf16[256,512]{1,0:T(8,128)(2,1)S(1)}, u32[]{:S(2)}, u32[]{:S(2)}) collective-permute-start(bf16[256,512]{1,0:T(8,128)(2,1)S(1)} %get-tuple-element.9), channel_id=1, source_target_pairs={{16,0},{17,1},{18,2},{19,3},{20,4},{21,5},{22,6},{23,7},{24,8},{25... | collective-permute-start | bytes 786440 | tf_op jit(solution)/shard_map/ppermute | solution.py:231
  50.4 13.2 %all-to-all-done = bf16[16,16,512]{2,1,0:T(8,128)(2,1)S(1)} async-done(((bf16[16,16,512]{2,1,0:T(8,128)(2,1)}), bf16[16,16,512]{2,1,0:T(8,128)(2,1)S(1)}, u32[]{:S(2)}, u32[]{:S(2)}) %all-to-all-start) | async-done | bytes 262176 | tf_op jit(solution)/shard_map/all_to_all | solution.py:195
  63.7 0.0 copy-done.5
  63.7 2.0 %shard_map.114 = bf16[256,512]{1,0:T(8,128)(2,1)} custom-call(bf16[256,512]{1,0:T(8,128)(2,1)S(1)} %copy-done.2, bf16[256,512]{1,0:T(8,128)(2,1)S(1)} %get-tuple-element.6.hidden_ref, bf16[256,512]{1,0:T(8,128)(2,1)S(1)} %bitcast.6, bf16[128,64]{1,0:T(8,128)(2,1)S(1)} %copy.12.mix_ref, bf16[2,2,128,128]{3,2,1,0:T(8,128)(2,1)S(1)} %copy-done.3, ...), custom_call_target="tpu_custom_call" | custom-call | flops 104857600 | bytes 1048576 | tf_op jit(solution)/shard_map/pallas_call | solution.py:163
  65.6 0.0 collective-permute-done.1.later_ref
  65.6 0.8 %shard_map.118 = bf16[256,512]{1,0:T(8,128)(2,1)} custom-call(bf16[256,512]{1,0:T(8,128)(2,1)S(1)} %copy-done.1, f32[256,512]{1,0:T(8,128)S(1)} %get-tuple-element.8.now_ref, bf16[256,512]{1,0:T(8,128)(2,1)S(1)} %collective-permute-done.1.later_ref), custom_call_target="tpu_custom_call" | custom-call | flops 1048576 | bytes 1048576 | tf_op jit(solution)/shard_map/pallas_call | solution.py:163
  (6 shorter events, 0.0 us)
Async XLA Ops:
  0.6 0.8 %copy-start.7 = (s32[16,16]{1,0:T(8,128)S(1)}, s32[16,16]{1,0:T(8,128)}, u32[]{:S(2)}) copy-start(s32[16,16]{1,0:T(8,128)} %count_ref.3) | copy-start | bytes 3076
  1.5 1.0 %copy-start = (bf16[256,512]{1,0:T(8,128)(2,1)S(1)}, bf16[256,512]{1,0:T(8,128)(2,1)}, u32[]{:S(2)}) copy-start(bf16[256,512]{1,0:T(8,128)(2,1)} %cot_ref.5) | copy-start | bytes 786436
  2.4 0.9 %copy-start.4 = (bf16[256,256]{1,0:T(8,128)(2,1)S(1)}, bf16[256,256]{1,0:T(8,128)(2,1)}, u32[]{:S(2)}) copy-start(bf16[256,256]{1,0:T(8,128)(2,1)} %values_ref.3) | copy-start | bytes 393220
  5.4 15.3 %copy-start.2 = (bf16[256,512]{1,0:T(8,128)(2,1)S(1)}, bf16[256,512]{1,0:T(8,128)(2,1)}, u32[]{:S(2)}) copy-start(bf16[256,512]{1,0:T(8,128)(2,1)} %series_ref.5) | copy-start | bytes 786436
  5.4 16.7 %copy-start.10 = (s32[1,16,16]{2,1,0:T(8,128)S(1)}, s32[1,16,16]{2,1,0:T(8,128)}, u32[]{:S(2)}) copy-start(s32[1,16,16]{2,1,0:T(8,128)} %param.16) | copy-start | bytes 3076
  5.4 26.5 %copy-start.6 = (bf16[128,128]{1,0:T(8,128)(2,1)S(1)}, bf16[128,128]{1,0:T(8,128)(2,1)}, u32[]{:S(2)}) copy-start(bf16[128,128]{1,0:T(8,128)(2,1)} %conv_ref.3) | copy-start | bytes 98308
  5.4 33.7 %all-to-all-start.1 = ((bf16[16,16,512]{2,1,0:T(8,128)(2,1)}), bf16[16,16,512]{2,1,0:T(8,128)(2,1)S(1)}, u32[]{:S(2)}, u32[]{:S(2)}) async-start(bf16[16,16,512]{2,1,0:T(8,128)(2,1)} %bitcast.3), calls=%async_computation.1 | async-start | bytes 524288 | tf_op jit(solution)/shard_map/all_to_all | solution.py:195
  20.8 11.2 %collective-permute-start = (bf16[256,512]{1,0:T(8,128)(2,1)S(1)}, bf16[256,512]{1,0:T(8,128)(2,1)S(1)}, u32[]{:S(2)}, u32[]{:S(2)}) collective-permute-start(bf16[256,512]{1,0:T(8,128)(2,1)S(1)} %copy-done.2), channel_id=1, source_target_pairs={{0,16},{1,17},{2,18},{3,19},{4,20},{5,21},{6,22},{7,23},{8,24},{9,... | collective-permute-start | bytes 786440 | tf_op jit(solution)/shard_map/ppermute | solution.py:198
  22.2 9.8 %copy-start.9 = (f32[128]{0:T(128)S(1)}, f32[128]{0:T(128)}, u32[]{:S(2)}) copy-start(f32[128]{0:T(128)} %param.12) | copy-start | bytes 1540
  39.1 6.3 %copy-start.1 = (bf16[256,512]{1,0:T(8,128)(2,1)S(1)}, bf16[256,512]{1,0:T(8,128)(2,1)}, u32[]{:S(2)}) copy-start(bf16[256,512]{1,0:T(8,128)(2,1)} %cot_ref.5) | copy-start | bytes 786436
  39.1 6.3 %copy-start.3 = (bf16[2,2,128,128]{3,2,1,0:T(8,128)(2,1)S(1)}, bf16[2,2,128,128]{3,2,1,0:T(8,128)(2,1)}, u32[]{:S(2)}) copy-start(bf16[2,2,128,128]{3,2,1,0:T(8,128)(2,1)} %local_ref.3) | copy-start | bytes 393220
  39.1 6.3 %copy-start.8 = (s32[2,2]{1,0:T(2,128)S(1)}, s32[2,2]{1,0:T(2,128)}, u32[]{:S(2)}) copy-start(s32[2,2]{1,0:T(2,128)} %blocks_ref.3) | copy-start | bytes 52
  39.1 24.5 %all-to-all-start = ((bf16[16,16,512]{2,1,0:T(8,128)(2,1)}), bf16[16,16,512]{2,1,0:T(8,128)(2,1)S(1)}, u32[]{:S(2)}, u32[]{:S(2)}) async-start(bf16[16,16,512]{2,1,0:T(8,128)(2,1)} %bitcast.1), calls=%async_computation | async-start | bytes 524288 | tf_op jit(solution)/shard_map/all_to_all | solution.py:195
  46.6 17.1 %copy-start.5 = (bf16[256,256]{1,0:T(8,128)(2,1)S(1)}, bf16[256,256]{1,0:T(8,128)(2,1)}, u32[]{:S(2)}) copy-start(bf16[256,256]{1,0:T(8,128)(2,1)} %values_ref.3) | copy-start | bytes 393220
  47.6 18.0 %collective-permute-start.1 = (bf16[256,512]{1,0:T(8,128)(2,1)S(1)}, bf16[256,512]{1,0:T(8,128)(2,1)S(1)}, u32[]{:S(2)}, u32[]{:S(2)}) collective-permute-start(bf16[256,512]{1,0:T(8,128)(2,1)S(1)} %get-tuple-element.9), channel_id=1, source_target_pairs={{16,0},{17,1},{18,2},{19,3},{20,4},{21,5},{22,6},{23,7},{24,8},{25... | collective-permute-start | bytes 786440 | tf_op jit(solution)/shard_map/ppermute | solution.py:231

commit v2 on v1

v2 whole, which is shorter than its diff:
```python
import jax
import jax.numpy as jnp
from jax import lax
from jax.experimental import pallas as pl
from jax.experimental.pallas import tpu as pltpu
from jax.sharding import PartitionSpec as P

C = 64
PAIR = 2 * C
F32 = jnp.float32
BF16 = jnp.bfloat16


def dot(a, b):
    return lax.dot_general(a, b, (((1,), (0,)), ((), ())), preferred_element_type=F32)


def dot_nt(a, b):
    return lax.dot_general(a, b, (((1,), (1,)), ((), ())), preferred_element_type=F32)


def dot_tn(a, b):
    return lax.dot_general(a, b, (((0,), (0,)), ((), ())), preferred_element_type=F32)


def iota(shape, dim):
    return lax.broadcasted_iota(jnp.int32, shape, dim)


def two_steps(weight):
    weight = weight.astype(F32)
    turned = pltpu.roll(weight, C, 1)
    low = iota(weight.shape, 1) < C
    even = jnp.concatenate([jnp.where(low, weight, 0.0), jnp.where(low, turned, 0.0)], axis=1)
    odd = jnp.concatenate([jnp.where(low, 0.0, turned), jnp.where(low, 0.0, weight)], axis=1)
    return jnp.concatenate([even, odd], axis=0).astype(BF16)


def conv_pair(conv_ref):
    return jnp.concatenate([two_steps(conv_ref[:C]), two_steps(conv_ref[C:])], axis=0)


def bias_pair(bias_ref):
    bias = bias_ref[...]
    turned = pltpu.roll(jnp.broadcast_to(bias, (8, PAIR)), C, 1)[:1]
    low = iota(bias.shape, 1) < C
    return jnp.concatenate([jnp.where(low, bias, turned), jnp.where(low, turned, bias)], axis=1)


def spread(table, slots):
    groups, cap = table.shape
    spot = iota((cap, slots), 1)
    place = jnp.where(lax.rem(spot, cap) == iota((cap, slots), 0), 1.0, 0.0).astype(BF16)
    wide = dot(table.astype(F32).astype(BF16), place)
    mine = iota((groups, slots), 1) // cap == iota((groups, slots), 0)
    return jnp.sum(jnp.where(mine, wide, 0.0), axis=0, keepdims=True)


def picker(rows_ref, nodes, slots):
    rows = spread(rows_ref[0], slots)
    return jnp.where(iota((nodes, slots), 0).astype(F32) == rows, 1.0, 0.0).astype(BF16)


def live_values(values_ref, count_ref):
    groups = count_ref.shape[0]
    slots = values_ref.shape[1]
    cap = slots // groups
    me = lax.axis_index("node")
    counts = count_ref[...].astype(F32)
    counts = jnp.where(iota(counts.shape, 1) == me, counts, 0.0)
    counts = jnp.sum(counts, axis=1, keepdims=True)
    column = iota((groups, slots), 1)
    mine = column // cap == iota((groups, slots), 0)
    limit = jnp.sum(jnp.where(mine, counts, 0.0), axis=0, keepdims=True)
    alive = lax.rem(column, cap)[:1].astype(F32) < limit
    return jnp.where(alive, values_ref[...].astype(F32), 0.0).astype(BF16)


def tanh_sigmoid(preact):
    filtered = jnp.tanh(preact[:, :PAIR])
    opened = 0.5 * jnp.tanh(0.5 * preact[:, PAIR:]) + 0.5
    return filtered, opened


def pairs(columns):
    return [slice(at, at + PAIR) for at in range(0, columns, PAIR)]


def wides(columns):
    return [slice(2 * at, 2 * at + 2 * PAIR) for at in range(0, columns, PAIR)]


def send_kernel(
    rows_hbm,
    series_hbm,
    mix_hbm,
    cot_hbm,
    count_hbm,
    values_hbm,
    out_hbm,
    rows_ref,
    series_ref,
    mix_ref,
    cot_ref,
    count_ref,
    values_ref,
    out_ref,
    came,
    gone,
):
    nodes, columns = series_ref.shape
    _, groups, cap, _ = out_ref.shape
    slots = groups * cap
    brought = [
        pltpu.make_async_copy(source, target, came.at[n])
        for n, (source, target) in enumerate(
            [
                (rows_hbm, rows_ref),
                (series_hbm, series_ref),
                (mix_hbm, mix_ref),
                (cot_hbm, cot_ref),
                (count_hbm, count_ref),
                (values_hbm, values_ref),
            ]
        )
    ]
    for copy in brought:
        copy.start()
    sent = [
        pltpu.make_async_copy(out_ref.at[n], out_hbm.at[:, pl.ds(n * cap, cap), :], gone.at[n])
        for n in range(2)
    ]
    brought[0].wait()
    pick = picker(rows_ref, nodes, slots)
    brought[1].wait()
    listed = dot_tn(pick, series_ref[...]).astype(BF16)
    out_ref[0] = listed.reshape(groups, cap, columns)
    sent[0].start()
    brought[2].wait()
    mix = two_steps(mix_ref[...])[:, PAIR:]
    brought[3].wait()
    mixed_grad = jnp.concatenate([dot(cot_ref[:, c], mix).astype(BF16) for c in pairs(columns)], axis=1)
    brought[4].wait()
    brought[5].wait()
    live = live_values(values_ref, count_ref)
    returned = dot_tn(live, mixed_grad).astype(BF16)
    out_ref[1] = returned.reshape(groups, cap, columns)
    sent[1].start()
    sent[0].wait()
    sent[1].wait()


def local_grad_kernel(
    cot_ref,
    mix_ref,
    local_ref,
    rows_ref,
    values_ref,
    count_ref,
    blocks_ref,
    out_ref,
    pick_ref,
    live_ref,
):
    nodes, slots = values_ref.shape
    pick_ref[...] = picker(rows_ref, nodes, slots)
    live_ref[...] = live_values(values_ref, count_ref)
    mix = two_steps(mix_ref[...])
    tiles, per_tile, size, _ = local_ref.shape
    kept = []
    for c in pairs(cot_ref.shape[1]):
        grads = dot(cot_ref[:, c], mix)
        out_ref[:, c] = grads[:, :PAIR]
        kept.append(grads[:, PAIR:].astype(BF16))
    mixed_grad = jnp.concatenate(kept, axis=1)
    for t in range(tiles):
        for b in range(per_tile):
            rows = pl.ds(pl.multiple_of(blocks_ref[t, b] * size, size), size)
            out_ref[rows, :] += dot_tn(local_ref[t, b], mixed_grad[t * size : (t + 1) * size])


def own_kernel(
    series_ref,
    delayed_ref,
    conv_ref,
    bias_ref,
    mix_ref,
    local_ref,
    blocks_ref,
    base_ref,
    slope_ref,
    weight_ref,
    bias_out_ref,
    mix_out_ref,
    hidden_ref,
):
    weight = conv_pair(conv_ref)
    bias = bias_pair(bias_ref)
    mix = two_steps(mix_ref[...])
    weight_ref[...] = weight
    bias_out_ref[...] = jnp.broadcast_to(bias, bias_out_ref.shape)
    mix_out_ref[...] = mix[:, PAIR:]
    tiles, per_tile, size, _ = local_ref.shape
    columns = series_ref.shape[1]
    for c, w in zip(pairs(columns), wides(columns)):
        stacked = jnp.concatenate([delayed_ref[:, c], series_ref[:, c]], axis=1)
        filtered, opened = tanh_sigmoid(dot(stacked, weight) + bias)
        hidden_ref[:, c] = (filtered * opened).astype(BF16)
        first = opened * (1.0 - filtered * filtered)
        second = filtered * opened * (1.0 - opened)
        slope_ref[:, w] = jnp.concatenate([first, second], axis=1)
    sums = []
    for t in range(tiles):
        total = None
        for b in range(per_tile):
            rows = pl.ds(pl.multiple_of(blocks_ref[t, b] * size, size), size)
            term = dot(local_ref[t, b], hidden_ref[rows, :])
            total = term if total is None else total + term
        sums.append(total.astype(BF16))
    local_sum = jnp.concatenate(sums, axis=0)
    for c in pairs(columns):
        both = jnp.concatenate([hidden_ref[:, c], local_sum[:, c]], axis=1)
        base_ref[:, c] = series_ref[:, c].astype(F32) + dot_nt(both, mix)


def gate_grad_kernel(got_ref, partial_ref, slope_ref, pick_ref, weight_ref, gate_ref, swap_ref):
    groups, both, columns = got_ref.shape
    cap = both // 2
    second_half = lax.axis_index("tm") >= lax.axis_size("tm") // 2
    back = got_ref[:, cap:, :].reshape(groups * cap, columns)
    upstream = (partial_ref[...] + dot(pick_ref[...], back)).astype(BF16).astype(F32)
    for c, w in zip(pairs(columns), wides(columns)):
        up = upstream[:, c]
        gate_ref[:, w] = (jnp.concatenate([up, up], axis=1) * slope_ref[:, w]).astype(BF16)

    @pl.when(second_half)
    def _():
        for c, w in zip(pairs(columns), wides(columns)):
            swap_ref[:, c] = dot_nt(gate_ref[:, w], weight_ref[:PAIR]).astype(BF16)

    @pl.when(jnp.logical_not(second_half))
    def _():
        swap_ref[...] = got_ref[:, :cap, :].reshape(groups * cap, columns)


def now_kernel(gate_ref, weight_ref, now_ref):
    columns = now_ref.shape[1]
    for c, w in zip(pairs(columns), wides(columns)):
        now_ref[:, c] = dot_nt(gate_ref[:, w], weight_ref[PAIR:])


def last_kernel(
    came_ref,
    got_ref,
    now_ref,
    live_ref,
    base_ref,
    cot_ref,
    weight_ref,
    bias_ref,
    mix_ref,
    out_ref,
    grad_ref,
):
    groups, both, columns = got_ref.shape
    cap = both // 2
    second_half = lax.axis_index("tm") >= lax.axis_size("tm") // 2
    came = came_ref[jnp.where(second_half, 0, 1)].astype(F32)
    later = jnp.where(second_half, 0.0, came)
    grad = (now_ref[...] + later).astype(BF16)
    grad_ref[...] = (cot_ref[...].astype(F32) + grad.astype(F32)).astype(BF16)
    before = jnp.where(second_half, came, 0.0).astype(BF16)
    listed = got_ref[:, :cap, :].reshape(groups * cap, columns)
    for c in pairs(columns):
        stacked = jnp.concatenate([before[:, c], listed[:, c]], axis=1)
        filtered, opened = tanh_sigmoid(dot(stacked, weight_ref[...]) + bias_ref[:1])
        hidden = (filtered * opened).astype(BF16)
        mixed = dot(live_ref[...], hidden).astype(BF16)
        out_ref[:, c] = (base_ref[:, c] + dot_nt(mixed, mix_ref[...])).astype(BF16)


VMEM = pl.BlockSpec(memory_space=pltpu.VMEM)
SMEM = pl.BlockSpec(memory_space=pltpu.SMEM)
HBM = pl.BlockSpec(memory_space=pltpu.HBM)


def call(kernel, outs, *args, scalars=(), ins=VMEM, out=VMEM, scratch=(), limit=32):
    many = isinstance(outs, tuple)
    return pl.pallas_call(
        kernel,
        out_shape=outs,
        in_specs=[SMEM if n in scalars else ins for n in range(len(args))],
        out_specs=tuple(out for _ in outs) if many else out,
        scratch_shapes=scratch,
        compiler_params=pltpu.CompilerParams(vmem_limit_bytes=limit << 20),
        cost_estimate=pl.CostEstimate(flops=1 << 27, bytes_accessed=1 << 21, transcendentals=0),
    )(*args)


def local(
    series,
    conv_weight,
    conv_bias,
    mix_weight,
    local_blocks,
    local_values,
    send_rows,
    send_count,
    remote_values,
    cotangent,
):
    nodes, columns = series.shape
    groups, cap = send_rows.shape[1:]
    slots = groups * cap
    places = lax.axis_size("tm")
    half = places // 2

    def shape(rows, cols, kind):
        return jax.ShapeDtypeStruct((rows, cols), kind)

    mix = mix_weight.T
    bias = conv_bias.reshape(1, -1)
    first = (send_rows, series, mix, cotangent, send_count, remote_values)
    send = call(
        send_kernel,
        jax.ShapeDtypeStruct((groups, 2 * cap, columns), BF16),
        *first,
        ins=HBM,
        out=HBM,
        limit=60,
        scratch=[pltpu.VMEM(a.shape, a.dtype) for a in first]
        + [
            pltpu.VMEM((2, groups, cap, columns), BF16),
            pltpu.SemaphoreType.DMA((len(first),)),
            pltpu.SemaphoreType.DMA((2,)),
        ],
    )
    got = lax.all_to_all(send, "node", 0, 0, tiled=True)
    delayed = lax.ppermute(series, "tm", [(i, i + half) for i in range(half)])
    partial, pick, live = call(
        local_grad_kernel,
        (shape(nodes, columns, F32), shape(nodes, slots, BF16), shape(nodes, slots, BF16)),
        cotangent,
        mix,
        local_values,
        send_rows,
        remote_values,
        send_count,
        local_blocks,
        scalars=(6,),
    )
    base, slope, weight, bias_wide, mix_mixed = call(
        own_kernel,
        (
            shape(nodes, columns, F32),
            shape(nodes, 2 * columns, F32),
            shape(2 * PAIR, 2 * PAIR, BF16),
            shape(8, 2 * PAIR, F32),
            shape(PAIR, PAIR, BF16),
        ),
        series,
        delayed,
        conv_weight,
        bias,
        mix,
        local_values,
        local_blocks,
        scalars=(6,),
        scratch=[pltpu.VMEM((nodes, columns), BF16)],
    )
    gate, swap = call(
        gate_grad_kernel,
        (shape(nodes, 2 * columns, BF16), shape(nodes, columns, BF16)),
        got,
        partial,
        slope,
        pick,
        weight,
    )
    came = lax.all_gather(swap, "tm", axis_index_groups=[[i, i + half] for i in range(half)])
    now = call(now_kernel, shape(nodes, columns, F32), gate, weight)
    return call(
        last_kernel,
        (shape(nodes, columns, BF16), shape(nodes, columns, BF16)),
        came,
        got,
        now,
        live,
        base,
        cotangent,
        weight,
        bias_wide,
        mix_mixed,
    )


def solution(mesh):
    in_specs = (
        P("node", "tm"),
        P(),
        P(),
        P(),
        P("node", None),
        P("node", None, None, None),
        P("node", None, None),
        P(),
        P("node", None),
        P("node", "tm"),
    )
    out_specs = (P("node", "tm"), P("node", "tm"))
    return jax.shard_map(local, mesh=mesh, in_specs=in_specs, out_specs=out_specs, check_vma=False)
```

time: 66.9 us -> 60.2 us (0.90)
  the two profiles are of different devices: /device:TPU:26 before, /device:TPU:30 now
where the time goes in v2:
time: 60.2 us; the launch traced here: 59.9 us
  waiting for transfers between devices  23.1 us (38%)
  starting transfers between devices  16.6 us (28%)
  blocking collectives  8.55 us (14%)
  Pallas kernels  8.09 us (13%)
  local copies, waits for them, and re-layouts  2.63 us (4%)
  between operations  0.85 us (1%)
    all_to_all x1, starting transfers between devices, local(): got = lax.all_to_all(send, 'node', 0, 0, tiled=True)  15.3 us
    all_to_all x1, waiting for transfers between devices, local(): got = lax.all_to_all(send, 'node', 0, 0, tiled=True)  15.1 us
    all_gather x1, blocking collectives, local(): lax.all_gather(swap, 'tm', axis_index_groups=[[i, i + half] for i in rang...  8.55 us
    pallas_call x6, Pallas kernels, call(): pl.pallas_call(kernel, out_shape=outs, in_specs=[SMEM if n in scalars els...  8.09 us
    ppermute x1, waiting for transfers between devices, local(): delayed = lax.ppermute(series, 'tm', [(i, i + half) for i in range(half)])  7.99 us
    unnamed x34, local copies, waits for them, and re-layouts  2.63 us
    ppermute x1, starting transfers between devices, local(): delayed = lax.ppermute(series, 'tm', [(i, i + half) for i in range(half)])  1.29 us
  transfers between devices with their start and end apart: 2, of which 2 were waited for; matrix products, arithmetic and copies ran while one was open for 0% of the time, Pallas kernels for 4%

profile of v2, /device:TPU:30, one launch (start us, length us, event | category | flops | bytes accessed | tf_op | source)
XLA Modules:
  0.0 59.9 jit_solution(1977560808320117889)
XLA Ops:
  0.6 2.6 %shard_map.113 = bf16[16,32,512]{2,1,0:T(8,128)(2,1)} custom-call(s32[1,16,16]{2,1,0:T(8,128)} %rows_ref.1, bf16[256,512]{1,0:T(8,128)(2,1)} %series_ref.1, bf16[64,128]{1,0:T(8,128)(2,1)} %bitcast.4, bf16[256,512]{1,0:T(8,128)(2,1)} %cot_ref.3, s32[16,16]{1,0:T(8,128)} %count_ref.1, bf16[256,256]{1,0:T(8,128)(2,1)} %values_ref.1), custom_call_target="tpu_custom_call" | custom-call | flops 134217728 | bytes 2097152 | tf_op jit(solution)/shard_map/pallas_call | solution.py:289
  3.3 0.0 copy-start.1
  3.3 0.0 copy-start
  3.3 0.0 copy-start.2
  3.3 0.0 copy-start.3
  3.3 0.0 copy-start.4
  3.3 0.0 copy-start.7
  3.3 0.0 copy-start.8
  3.4 0.0 copy-start.14
  3.4 15.3 %all-to-all-start = ((bf16[16,32,512]{2,1,0:T(8,128)(2,1)}), bf16[16,32,512]{2,1,0:T(8,128)(2,1)S(1)}, u32[]{:S(2)}, u32[]{:S(2)}) async-start(bf16[16,32,512]{2,1,0:T(8,128)(2,1)} %shard_map.113), calls=%async_computation | async-start | bytes 1048576 | tf_op jit(solution)/shard_map/all_to_all | solution.py:338
  18.7 0.0 copy-start.9
  18.7 1.3 %collective-permute-start = (bf16[256,512]{1,0:T(8,128)(2,1)S(1)}, bf16[256,512]{1,0:T(8,128)(2,1)S(1)}, u32[]{:S(2)}, u32[]{:S(2)}) collective-permute-start(bf16[256,512]{1,0:T(8,128)(2,1)S(1)} %copy-done.1), channel_id=1, source_target_pairs={{0,16},{1,17},{2,18},{3,19},{4,20},{5,21},{6,22},{7,23},{8,24},{9,... | collective-permute-start | bytes 786440 | tf_op jit(solution)/shard_map/ppermute | solution.py:339
  20.0 0.0 copy-done
  20.1 0.0 copy-done.2
  20.1 0.0 copy-done.3
  20.1 0.0 copy-done.4
  20.1 0.0 copy-done.7
  20.1 1.1 %shard_map.114 = (f32[256,512]{1,0:T(8,128)S(1)}, bf16[256,256]{1,0:T(8,128)(2,1)S(1)}, bf16[256,256]{1,0:T(8,128)(2,1)S(1)}) custom-call(bf16[256,512]{1,0:T(8,128)(2,1)S(1)} %copy-done, bf16[64,128]{1,0:T(8,128)(2,1)S(1)} %bitcast.5, bf16[2,2,128,128]{3,2,1,0:T(8,128)(2,1)S(1)} %copy-done.3, s32[1,16,16]{2,1,0:T(8,128)S(1)} %copy-done.7, ...), custom_call_target="tpu_custom_call" | custom-call | flops 134217728 | bytes 2097152 | tf_op jit(solution)/shard_map/pallas_call | solution.py:289
  21.3 0.0 copy-start.5
  21.3 0.6 %copy-done.5 = bf16[256,256]{1,0:T(8,128)(2,1)} copy-done((bf16[256,256]{1,0:T(8,128)(2,1)}, bf16[256,256]{1,0:T(8,128)(2,1)S(1)}, u32[]{:S(2)}) %copy-start.5) | copy-done | bytes 131096
  21.9 8.0 %collective-permute-done.delayed_ref = bf16[256,512]{1,0:T(8,128)(2,1)S(1)} collective-permute-done((bf16[256,512]{1,0:T(8,128)(2,1)S(1)}, bf16[256,512]{1,0:T(8,128)(2,1)S(1)}, u32[]{:S(2)}, u32[]{:S(2)}) %collective-permute-start) | collective-permute-done | bytes 262176 | tf_op jit(solution)/shard_map/ppermute | solution.py:339
  29.9 1.5 %shard_map.115 = (f32[256,512]{1,0:T(8,128)S(1)}, f32[256,1024]{1,0:T(8,128)S(1)}, bf16[256,256]{1,0:T(8,128)(2,1)S(1)}, f32[8,256]{1,0:T(8,128)S(1)}, bf16[128,128]{1,0:T(8,128)(2,1)S(1)}) custom-call(bf16[256,512]{1,0:T(8,128)(2,1)S(1)} %copy-done.1, bf16[256,512]{1,0:T(8,128)(2,1)S(1)} %collective-permute-done.delayed_ref, ...), custom_call_target="tpu_custom_call" | custom-call | flops 134217728 | bytes 2097152 | tf_op jit(solution)/shard_map/pallas_call | solution.py:289
  31.5 0.0 copy-start.10
  31.5 0.6 %copy-done.10 = bf16[128,128]{1,0:T(8,128)(2,1)} copy-done((bf16[128,128]{1,0:T(8,128)(2,1)}, bf16[128,128]{1,0:T(8,128)(2,1)S(1)}, u32[]{:S(2)}) %copy-start.10) | copy-done | bytes 32792
  32.1 0.6 copy-done.12
  32.7 15.1 %all-to-all-done.got_ref = bf16[16,32,512]{2,1,0:T(8,128)(2,1)S(1)} async-done(((bf16[16,32,512]{2,1,0:T(8,128)(2,1)}), bf16[16,32,512]{2,1,0:T(8,128)(2,1)S(1)}, u32[]{:S(2)}, u32[]{:S(2)}) %all-to-all-start) | async-done | bytes 524320 | tf_op jit(solution)/shard_map/all_to_all | solution.py:338
  47.8 0.6 shard_map.116
  48.4 8.6 %all-gather = bf16[512,512]{1,0:T(8,128)(2,1)S(1)} all-gather(bf16[256,512]{1,0:T(8,128)(2,1)S(1)} %get-tuple-element.16), channel_id=2, replica_groups={{0,16},{1,17},{2,18},{3,19},{4,20},{5,21},{6,22},{7,23},{8,24},{9,25},{..., dimensions={0}, use_global_device_ids=true | all-gather | bytes 786432 | tf_op jit(solution)/shard_map/all_gather | solution.py:380
  56.9 0.3 shard_map.117.now_ref
  57.2 0.6 %copy-done.6 = bf16[256,256]{1,0:T(8,128)(2,1)S(1)} copy-done((bf16[256,256]{1,0:T(8,128)(2,1)S(1)}, bf16[256,256]{1,0:T(8,128)(2,1)}, u32[]{:S(2)}) %copy-start.6) | copy-done | bytes 131096
  57.8 0.1 copy-done.13
  57.9 1.9 %shard_map.118 = (bf16[256,512]{1,0:T(8,128)(2,1)}, bf16[256,512]{1,0:T(8,128)(2,1)}) custom-call(bf16[2,256,512]{2,1,0:T(8,128)(2,1)S(1)} %bitcast.3, bf16[16,32,512]{2,1,0:T(8,128)(2,1)S(1)} %all-to-all-done.got_ref, f32[256,512]{1,0:T(8,128)S(1)} %shard_map.117.now_ref, bf16[256,256]{1,0:T(8,128)(2,1)S(1)} %copy-done.6, ...), custom_call_target="tpu_custom_call" | custom-call | flops 134217728 | bytes 2097152 | tf_op jit(solution)/shard_map/pallas_call | solution.py:289
  (13 shorter events, 0.0 us)
Async XLA Ops:
  3.3 15.4 %copy-start.1 = (bf16[256,512]{1,0:T(8,128)(2,1)S(1)}, bf16[256,512]{1,0:T(8,128)(2,1)}, u32[]{:S(2)}) copy-start(bf16[256,512]{1,0:T(8,128)(2,1)} %series_ref.1) | copy-start | bytes 786436
  3.3 16.8 %copy-start = (bf16[256,512]{1,0:T(8,128)(2,1)S(1)}, bf16[256,512]{1,0:T(8,128)(2,1)}, u32[]{:S(2)}) copy-start(bf16[256,512]{1,0:T(8,128)(2,1)} %cot_ref.3) | copy-start | bytes 786436
  3.3 16.8 %copy-start.2 = (bf16[256,256]{1,0:T(8,128)(2,1)S(1)}, bf16[256,256]{1,0:T(8,128)(2,1)}, u32[]{:S(2)}) copy-start(bf16[256,256]{1,0:T(8,128)(2,1)} %values_ref.1) | copy-start | bytes 393220
  3.3 16.8 %copy-start.3 = (bf16[2,2,128,128]{3,2,1,0:T(8,128)(2,1)S(1)}, bf16[2,2,128,128]{3,2,1,0:T(8,128)(2,1)}, u32[]{:S(2)}) copy-start(bf16[2,2,128,128]{3,2,1,0:T(8,128)(2,1)} %local_ref.3) | copy-start | bytes 393220
  3.3 16.8 %copy-start.4 = (bf16[128,64]{0,1:T(8,128)(2,1)S(1)}, bf16[128,64]{0,1:T(8,128)(2,1)}, u32[]{:S(2)}) copy-start(bf16[128,64]{0,1:T(8,128)(2,1)} %param.13) | copy-start | bytes 49156
  3.3 16.7 %copy-start.7 = (s32[1,16,16]{2,1,0:T(8,128)S(1)}, s32[1,16,16]{2,1,0:T(8,128)}, u32[]{:S(2)}) copy-start(s32[1,16,16]{2,1,0:T(8,128)} %rows_ref.1) | copy-start | bytes 3076
  3.3 16.7 %copy-start.8 = (s32[16,16]{1,0:T(8,128)S(1)}, s32[16,16]{1,0:T(8,128)}, u32[]{:S(2)}) copy-start(s32[16,16]{1,0:T(8,128)} %count_ref.1) | copy-start | bytes 3076
  3.4 16.7 %copy-start.14 = (s32[2,2]{1,0:T(2,128)S(1)}, s32[2,2]{1,0:T(2,128)}, u32[]{:S(2)}) copy-start(s32[2,2]{1,0:T(2,128)} %blocks_ref.3) | copy-start | bytes 52
  3.4 44.4 %all-to-all-start = ((bf16[16,32,512]{2,1,0:T(8,128)(2,1)}), bf16[16,32,512]{2,1,0:T(8,128)(2,1)S(1)}, u32[]{:S(2)}, u32[]{:S(2)}) async-start(bf16[16,32,512]{2,1,0:T(8,128)(2,1)} %shard_map.113), calls=%async_computation | async-start | bytes 1048576 | tf_op jit(solution)/shard_map/all_to_all | solution.py:338
  18.7 11.2 %copy-start.9 = (bf16[128,128]{1,0:T(8,128)(2,1)S(1)}, bf16[128,128]{1,0:T(8,128)(2,1)}, u32[]{:S(2)}) copy-start(bf16[128,128]{1,0:T(8,128)(2,1)} %conv_ref.1) | copy-start | bytes 98308
  18.7 11.2 %collective-permute-start = (bf16[256,512]{1,0:T(8,128)(2,1)S(1)}, bf16[256,512]{1,0:T(8,128)(2,1)S(1)}, u32[]{:S(2)}, u32[]{:S(2)}) collective-permute-start(bf16[256,512]{1,0:T(8,128)(2,1)S(1)} %copy-done.1), channel_id=1, source_target_pairs={{0,16},{1,17},{2,18},{3,19},{4,20},{5,21},{6,22},{7,23},{8,24},{9,... | collective-permute-start | bytes 786440 | tf_op jit(solution)/shard_map/ppermute | solution.py:339
  21.3 0.7 %copy-start.5 = (bf16[256,256]{1,0:T(8,128)(2,1)}, bf16[256,256]{1,0:T(8,128)(2,1)S(1)}, u32[]{:S(2)}) copy-start(bf16[256,256]{1,0:T(8,128)(2,1)S(1)} %get-tuple-element.18.live_ref) | copy-start | bytes 393220
  21.9 8.0 %copy-start.15 = (s32[2,2]{1,0:T(2,128)S(1)}, s32[2,2]{1,0:T(2,128)}, u32[]{:S(2)}) copy-start(s32[2,2]{1,0:T(2,128)} %blocks_ref.3) | copy-start | bytes 52
  21.9 8.0 %copy-start.16 = (f32[128]{0:T(128)S(1)}, f32[128]{0:T(128)}, u32[]{:S(2)}) copy-start(f32[128]{0:T(128)} %param.12) | copy-start | bytes 1540
  31.5 0.6 %copy-start.10 = (bf16[128,128]{1,0:T(8,128)(2,1)}, bf16[128,128]{1,0:T(8,128)(2,1)S(1)}, u32[]{:S(2)}) copy-start(bf16[128,128]{1,0:T(8,128)(2,1)S(1)} %get-tuple-element.21.mix_ref) | copy-start | bytes 98308
  32.1 0.6 copy-start.12
  56.9 0.9 %copy-start.6 = (bf16[256,256]{1,0:T(8,128)(2,1)S(1)}, bf16[256,256]{1,0:T(8,128)(2,1)}, u32[]{:S(2)}) copy-start(bf16[256,256]{1,0:T(8,128)(2,1)} %copy-done.5) | copy-start | bytes 393220
  56.9 0.9 %copy-start.11 = (bf16[128,128]{1,0:T(8,128)(2,1)S(1)}, bf16[128,128]{1,0:T(8,128)(2,1)}, u32[]{:S(2)}) copy-start(bf16[128,128]{1,0:T(8,128)(2,1)} %copy-done.10) | copy-start | bytes 98308
  57.2 0.7 %copy-start.13 = (f32[8,256]{1,0:T(8,128)S(1)}, f32[8,256]{1,0:T(8,128)}, u32[]{:S(2)}) copy-start(f32[8,256]{1,0:T(8,128)} %copy-done.12) | copy-start | bytes 24580

commit v3 on v2

--- a/solution.py
+++ b/solution.py
@@ -9,6 +9,7 @@
 PAIR = 2 * C
 F32 = jnp.float32
 BF16 = jnp.bfloat16
+FIRST = 12
 
 
 def dot(a, b):
@@ -74,6 +75,11 @@
     limit = jnp.sum(jnp.where(mine, counts, 0.0), axis=0, keepdims=True)
     alive = lax.rem(column, cap)[:1].astype(F32) < limit
     return jnp.where(alive, values_ref[...].astype(F32), 0.0).astype(BF16)
+
+
+def turned(blocks, first):
+    first = first % blocks.shape[0]
+    return jnp.concatenate([blocks[first:], blocks[:first]], axis=0) if first else blocks
 
 
 def tanh_sigmoid(preact):
@@ -130,21 +136,17 @@
         pltpu.make_async_copy(out_ref.at[n], out_hbm.at[:, pl.ds(n * cap, cap), :], gone.at[n])
         for n in range(2)
     ]
-    brought[0].wait()
+    for copy in brought:
+        copy.wait()
     pick = picker(rows_ref, nodes, slots)
-    brought[1].wait()
+    live = live_values(values_ref, count_ref)
+    mix = two_steps(mix_ref[...])[:, PAIR:]
+    mixed_grad = jnp.concatenate([dot(cot_ref[:, c], mix).astype(BF16) for c in pairs(columns)], axis=1)
     listed = dot_tn(pick, series_ref[...]).astype(BF16)
-    out_ref[0] = listed.reshape(groups, cap, columns)
+    out_ref[0] = turned(listed.reshape(groups, cap, columns), FIRST)
     sent[0].start()
-    brought[2].wait()
-    mix = two_steps(mix_ref[...])[:, PAIR:]
-    brought[3].wait()
-    mixed_grad = jnp.concatenate([dot(cot_ref[:, c], mix).astype(BF16) for c in pairs(columns)], axis=1)
-    brought[4].wait()
-    brought[5].wait()
-    live = live_values(values_ref, count_ref)
     returned = dot_tn(live, mixed_grad).astype(BF16)
-    out_ref[1] = returned.reshape(groups, cap, columns)
+    out_ref[1] = turned(returned.reshape(groups, cap, columns), FIRST)
     sent[1].start()
     sent[0].wait()
     sent[1].wait()
@@ -159,12 +161,11 @@
     count_ref,
     blocks_ref,
     out_ref,
-    pick_ref,
-    live_ref,
+    slots_ref,
 ):
     nodes, slots = values_ref.shape
-    pick_ref[...] = picker(rows_ref, nodes, slots)
-    live_ref[...] = live_values(values_ref, count_ref)
+    slots_ref[:, :slots] = picker(rows_ref, nodes, slots)
+    slots_ref[:, slots:] = live_values(values_ref, count_ref)
     mix = two_steps(mix_ref[...])
     tiles, per_tile, size, _ = local_ref.shape
     kept = []
@@ -190,16 +191,13 @@
     base_ref,
     slope_ref,
     weight_ref,
-    bias_out_ref,
-    mix_out_ref,
     hidden_ref,
 ):
     weight = conv_pair(conv_ref)
     bias = bias_pair(bias_ref)
     mix = two_steps(mix_ref[...])
-    weight_ref[...] = weight
-    bias_out_ref[...] = jnp.broadcast_to(bias, bias_out_ref.shape)
-    mix_out_ref[...] = mix[:, PAIR:]
+    weight_ref[: 2 * PAIR] = weight
+    weight_ref[2 * PAIR :] = mix
     tiles, per_tile, size, _ = local_ref.shape
     columns = series_ref.shape[1]
     for c, w in zip(pairs(columns), wides(columns)):
@@ -223,12 +221,12 @@
         base_ref[:, c] = series_ref[:, c].astype(F32) + dot_nt(both, mix)
 
 
-def gate_grad_kernel(got_ref, partial_ref, slope_ref, pick_ref, weight_ref, gate_ref, swap_ref):
+def gate_grad_kernel(got_ref, partial_ref, slope_ref, slots_ref, weight_ref, gate_ref, swap_ref):
     groups, both, columns = got_ref.shape
     cap = both // 2
     second_half = lax.axis_index("tm") >= lax.axis_size("tm") // 2
-    back = got_ref[:, cap:, :].reshape(groups * cap, columns)
-    upstream = (partial_ref[...] + dot(pick_ref[...], back)).astype(BF16).astype(F32)
+    back = turned(got_ref[:, cap:, :], -FIRST).reshape(groups * cap, columns)
+    upstream = (partial_ref[...] + dot(slots_ref[:, : groups * cap], back)).astype(BF16).astype(F32)
     for c, w in zip(pairs(columns), wides(columns)):
         up = upstream[:, c]
         gate_ref[:, w] = (jnp.concatenate([up, up], axis=1) * slope_ref[:, w]).astype(BF16)
@@ -240,43 +238,57 @@
 
     @pl.when(jnp.logical_not(second_half))
     def _():
-        swap_ref[...] = got_ref[:, :cap, :].reshape(groups * cap, columns)
-
-
-def now_kernel(gate_ref, weight_ref, now_ref):
-    columns = now_ref.shape[1]
-    for c, w in zip(pairs(columns), wides(columns)):
-        now_ref[:, c] = dot_nt(gate_ref[:, w], weight_ref[PAIR:])
+        swap_ref[...] = turned(got_ref[:, :cap, :], -FIRST).reshape(groups * cap, columns)
 
 
 def last_kernel(
     came_ref,
     got_ref,
-    now_ref,
-    live_ref,
+    gate_ref,
+    slots_ref,
     base_ref,
     cot_ref,
     weight_ref,
     bias_ref,
-    mix_ref,
+    out_hbm,
+    grad_hbm,
     out_ref,
     grad_ref,
+    gone,
 ):
     groups, both, columns = got_ref.shape
     cap = both // 2
+    slots = groups * cap
+    nodes = cot_ref.shape[0]
     second_half = lax.axis_index("tm") >= lax.axis_size("tm") // 2
     came = came_ref[jnp.where(second_half, 0, 1)].astype(F32)
     later = jnp.where(second_half, 0.0, came)
-    grad = (now_ref[...] + later).astype(BF16)
-    grad_ref[...] = (cot_ref[...].astype(F32) + grad.astype(F32)).astype(BF16)
+    for c, w in zip(pairs(columns), wides(columns)):
+        grad = (dot_nt(gate_ref[:, w], weight_ref[PAIR : 2 * PAIR]) + later[:, c]).astype(BF16)
+        grad_ref[:, c] = (cot_ref[:, c].astype(F32) + grad.astype(F32)).astype(BF16)
+    grad_copy = pltpu.make_async_copy(grad_ref, grad_hbm, gone.at[0])
+    grad_copy.start()
     before = jnp.where(second_half, came, 0.0).astype(BF16)
-    listed = got_ref[:, :cap, :].reshape(groups * cap, columns)
+    listed = turned(got_ref[:, :cap, :], -FIRST).reshape(slots, columns)
+    bias = bias_pair(bias_ref)
+    kept = []
     for c in pairs(columns):
         stacked = jnp.concatenate([before[:, c], listed[:, c]], axis=1)
-        filtered, opened = tanh_sigmoid(dot(stacked, weight_ref[...]) + bias_ref[:1])
-        hidden = (filtered * opened).astype(BF16)
-        mixed = dot(live_ref[...], hidden).astype(BF16)
-        out_ref[:, c] = (base_ref[:, c] + dot_nt(mixed, mix_ref[...])).astype(BF16)
+        filtered, opened = tanh_sigmoid(dot(stacked, weight_ref[: 2 * PAIR]) + bias)
+        kept.append((filtered * opened).astype(BF16))
+    hidden = jnp.concatenate(kept, axis=1)
+    copies = []
+    for n in range(2):
+        rows = pl.ds(n * (nodes // 2), nodes // 2)
+        mixed = dot(slots_ref[rows, slots:], hidden).astype(BF16)
+        for c in pairs(columns):
+            added = dot_nt(mixed[:, c], weight_ref[2 * PAIR :, PAIR:])
+            out_ref[rows, c] = (base_ref[rows, c] + added).astype(BF16)
+        copies.append(pltpu.make_async_copy(out_ref.at[rows], out_hbm.at[rows], gone.at[n + 1]))
+        copies[n].start()
+    grad_copy.wait()
+    for copy in copies:
+        copy.wait()
 
 
 VMEM = pl.BlockSpec(memory_space=pltpu.VMEM)
@@ -335,11 +347,12 @@
             pltpu.SemaphoreType.DMA((2,)),
         ],
     )
-    got = lax.all_to_all(send, "node", 0, 0, tiled=True)
+    order = [(FIRST + k) % groups for k in range(groups)]
+    got = lax.all_to_all(send, "node", 0, 0, axis_index_groups=[order], tiled=True)
     delayed = lax.ppermute(series, "tm", [(i, i + half) for i in range(half)])
-    partial, pick, live = call(
+    partial, picked_live = call(
         local_grad_kernel,
-        (shape(nodes, columns, F32), shape(nodes, slots, BF16), shape(nodes, slots, BF16)),
+        (shape(nodes, columns, F32), shape(nodes, 2 * slots, BF16)),
         cotangent,
         mix,
         local_values,
@@ -349,15 +362,9 @@
         local_blocks,
         scalars=(6,),
     )
-    base, slope, weight, bias_wide, mix_mixed = call(
+    base, slope, weight = call(
         own_kernel,
-        (
-            shape(nodes, columns, F32),
-            shape(nodes, 2 * columns, F32),
-            shape(2 * PAIR, 2 * PAIR, BF16),
-            shape(8, 2 * PAIR, F32),
-            shape(PAIR, PAIR, BF16),
-        ),
+        (shape(nodes, columns, F32), shape(nodes, 2 * columns, F32), shape(3 * PAIR, 2 * PAIR, BF16)),
         series,
         delayed,
         conv_weight,
@@ -374,23 +381,27 @@
         got,
         partial,
         slope,
-        pick,
+        picked_live,
         weight,
     )
     came = lax.all_gather(swap, "tm", axis_index_groups=[[i, i + half] for i in range(half)])
-    now = call(now_kernel, shape(nodes, columns, F32), gate, weight)
     return call(
         last_kernel,
         (shape(nodes, columns, BF16), shape(nodes, columns, BF16)),
         came,
         got,
-        now,
-        live,
+        gate,
+        picked_live,
         base,
         cotangent,
         weight,
-        bias_wide,
-        mix_mixed,
+        bias,
+        out=HBM,
+        scratch=[
+            pltpu.VMEM((nodes, columns), BF16),
+            pltpu.VMEM((nodes, columns), BF16),
+            pltpu.SemaphoreType.DMA((3,)),
+        ],
     )
 
 

time: 60.2 us -> 56.6 us (0.940)
  the two profiles are of different devices: /device:TPU:30 before, /device:TPU:54 now
where the time goes in v3:
time: 56.6 us; the launch traced here: 56.3 us
  waiting for transfers between devices  22 us (39%)
  starting transfers between devices  16.7 us (30%)
  blocking collectives  8.68 us (15%)
  Pallas kernels  7.28 us (13%)
  local copies, waits for them, and re-layouts  0.87 us (2%)
  between operations  0.82 us (1%)
    all_to_all x1, starting transfers between devices, local(): lax.all_to_all(send, 'node', 0, 0, axis_index_groups=[order], tiled=True)  15.4 us
    all_to_all x1, waiting for transfers between devices, local(): lax.all_to_all(send, 'node', 0, 0, axis_index_groups=[order], tiled=True)  13.7 us
    all_gather x1, blocking collectives, local(): lax.all_gather(swap, 'tm', axis_index_groups=[[i, i + half] for i in rang...  8.68 us
    ppermute x1, waiting for transfers between devices, local(): delayed = lax.ppermute(series, 'tm', [(i, i + half) for i in range(half)])  8.34 us
    pallas_call x5, Pallas kernels, call(): pl.pallas_call(kernel, out_shape=outs, in_specs=[SMEM if n in scalars els...  7.28 us
    ppermute x1, starting transfers between devices, local(): delayed = lax.ppermute(series, 'tm', [(i, i + half) for i in range(half)])  1.29 us
  transfers between devices with their start and end apart: 2, of which 2 were waited for; matrix products, arithmetic and copies ran while one was open for 0% of the time, Pallas kernels for 5%

profile of v3, /device:TPU:54, one launch (start us, length us, event | category | flops | bytes accessed | tf_op | source)
XLA Modules:
  0.0 56.3 jit_solution(14570112361718837201)
XLA Ops:
  0.6 2.4 %shard_map.113 = bf16[16,32,512]{2,1,0:T(8,128)(2,1)} custom-call(s32[1,16,16]{2,1,0:T(8,128)} %rows_ref.1, bf16[256,512]{1,0:T(8,128)(2,1)} %series_ref.1, bf16[64,128]{1,0:T(8,128)(2,1)} %bitcast.4, bf16[256,512]{1,0:T(8,128)(2,1)} %cot_ref.3, s32[16,16]{1,0:T(8,128)} %count_ref.1, bf16[256,256]{1,0:T(8,128)(2,1)} %values_ref.1), custom_call_target="tpu_custom_call" | custom-call | flops 134217728 | bytes 2097152 | tf_op jit(solution)/shard_map/pallas_call | solution.py:301
  3.1 0.0 copy-start.1
  3.1 0.0 copy-start
  3.1 0.0 copy-start.2
  3.1 0.0 copy-start.3
  3.1 0.0 copy-start.6
  3.1 0.0 copy-start.7
  3.2 0.0 copy-start.8
  3.2 0.0 copy-start.10
  3.2 15.4 %all-to-all-start = ((bf16[16,32,512]{2,1,0:T(8,128)(2,1)}), bf16[16,32,512]{2,1,0:T(8,128)(2,1)S(1)}, u32[]{:S(2)}, u32[]{:S(2)}) async-start(bf16[16,32,512]{2,1,0:T(8,128)(2,1)} %shard_map.113), calls=%async_computation | async-start | bytes 1048576 | tf_op jit(solution)/shard_map/all_to_all | solution.py:351
  18.5 0.0 copy-done.1
  18.5 0.0 copy-start.9
  18.6 1.3 %collective-permute-start = (bf16[256,512]{1,0:T(8,128)(2,1)S(1)}, bf16[256,512]{1,0:T(8,128)(2,1)S(1)}, u32[]{:S(2)}, u32[]{:S(2)}) collective-permute-start(bf16[256,512]{1,0:T(8,128)(2,1)S(1)} %copy-done.1), channel_id=1, source_target_pairs={{0,16},{1,17},{2,18},{3,19},{4,20},{5,21},{6,22},{7,23},{8,24},{9,... | collective-permute-start | bytes 786440 | tf_op jit(solution)/shard_map/ppermute | solution.py:352
  19.9 0.0 copy-done
  19.9 0.0 copy-done.2
  19.9 0.0 copy-done.3
  19.9 0.0 copy-done.6
  19.9 0.0 copy-done.7
  19.9 0.0 copy-done.8
  19.9 0.0 copy-done.10
  19.9 1.1 %shard_map.114 = (f32[256,512]{1,0:T(8,128)S(1)}, bf16[256,512]{1,0:T(8,128)(2,1)S(1)}) custom-call(bf16[256,512]{1,0:T(8,128)(2,1)S(1)} %copy-done, bf16[64,128]{1,0:T(8,128)(2,1)S(1)} %bitcast.5, bf16[2,2,128,128]{3,2,1,0:T(8,128)(2,1)S(1)} %copy-done.3, s32[1,16,16]{2,1,0:T(8,128)S(1)} %copy-done.7, bf16[256,256]{1,0:T(8,128)(2,1)S(1)} %copy-done.2, ...), custom_call_target="tpu_custom_call" | custom-call | flops 134217728 | bytes 2097152 | tf_op jit(solution)/shard_map/pallas_call | solution.py:301
  21.1 0.0 copy-start.11
  21.1 8.3 %collective-permute-done.delayed_ref = bf16[256,512]{1,0:T(8,128)(2,1)S(1)} collective-permute-done((bf16[256,512]{1,0:T(8,128)(2,1)S(1)}, bf16[256,512]{1,0:T(8,128)(2,1)S(1)}, u32[]{:S(2)}, u32[]{:S(2)}) %collective-permute-start) | collective-permute-done | bytes 262176 | tf_op jit(solution)/shard_map/ppermute | solution.py:352
  29.4 0.0 copy-done.9
  29.4 0.0 copy-done.11
  29.4 1.5 %shard_map.115 = (f32[256,512]{1,0:T(8,128)S(1)}, f32[256,1024]{1,0:T(8,128)S(1)}, bf16[384,256]{1,0:T(8,128)(2,1)S(1)}) custom-call(bf16[256,512]{1,0:T(8,128)(2,1)S(1)} %copy-done.1, bf16[256,512]{1,0:T(8,128)(2,1)S(1)} %collective-permute-done.delayed_ref, bf16[128,128]{1,0:T(8,128)(2,1)S(1)} %copy-done.9, f32[1,128]{1,0:T(1,128)S(1)} %bitcast.7, ...), custom_call_target="tpu_custom_call" | custom-call | flops 134217728 | bytes 2097152 | tf_op jit(solution)/shard_map/pallas_call | solution.py:301
  31.0 0.8 %copy-done.4 = f32[256,512]{1,0:T(8,128)} copy-done((f32[256,512]{1,0:T(8,128)}, f32[256,512]{1,0:T(8,128)S(1)}, u32[]{:S(2)}) %copy-start.4) | copy-done | bytes 524312
  31.8 13.7 %all-to-all-done.got_ref = bf16[16,32,512]{2,1,0:T(8,128)(2,1)S(1)} async-done(((bf16[16,32,512]{2,1,0:T(8,128)(2,1)}), bf16[16,32,512]{2,1,0:T(8,128)(2,1)S(1)}, u32[]{:S(2)}, u32[]{:S(2)}) %all-to-all-start) | async-done | bytes 524320 | tf_op jit(solution)/shard_map/all_to_all | solution.py:351
  45.5 0.6 shard_map.116
  46.0 8.7 %all-gather = bf16[512,512]{1,0:T(8,128)(2,1)S(1)} all-gather(bf16[256,512]{1,0:T(8,128)(2,1)S(1)} %get-tuple-element.13), channel_id=2, replica_groups={{0,16},{1,17},{2,18},{3,19},{4,20},{5,21},{6,22},{7,23},{8,24},{9,25},{..., dimensions={0}, use_global_device_ids=true | all-gather | bytes 786432 | tf_op jit(solution)/shard_map/all_gather | solution.py:387
  54.7 0.0 copy-done.5
  54.7 1.6 %shard_map.117 = (bf16[256,512]{1,0:T(8,128)(2,1)}, bf16[256,512]{1,0:T(8,128)(2,1)}) custom-call(bf16[2,256,512]{2,1,0:T(8,128)(2,1)S(1)} %bitcast.3, bf16[16,32,512]{2,1,0:T(8,128)(2,1)S(1)} %all-to-all-done.got_ref, bf16[256,1024]{1,0:T(8,128)(2,1)S(1)} %get-tuple-element.14.gate_ref, bf16[256,512]{1,0:T(8,128)(2,1)S(1)} %get-tuple-element.11.slots_ref, ...), custom_call_target="tpu_custom_call" | custom-call | flops 134217728 | bytes 2097152 | tf_op jit(solution)/shard_map/pallas_call | solution.py:301
  (2 shorter events, 0.0 us)
Async XLA Ops:
  3.1 15.5 %copy-start.1 = (bf16[256,512]{1,0:T(8,128)(2,1)S(1)}, bf16[256,512]{1,0:T(8,128)(2,1)}, u32[]{:S(2)}) copy-start(bf16[256,512]{1,0:T(8,128)(2,1)} %series_ref.1) | copy-start | bytes 786436
  3.1 16.8 %copy-start = (bf16[256,512]{1,0:T(8,128)(2,1)S(1)}, bf16[256,512]{1,0:T(8,128)(2,1)}, u32[]{:S(2)}) copy-start(bf16[256,512]{1,0:T(8,128)(2,1)} %cot_ref.3) | copy-start | bytes 786436
  3.1 16.8 %copy-start.2 = (bf16[256,256]{1,0:T(8,128)(2,1)S(1)}, bf16[256,256]{1,0:T(8,128)(2,1)}, u32[]{:S(2)}) copy-start(bf16[256,256]{1,0:T(8,128)(2,1)} %values_ref.1) | copy-start | bytes 393220
  3.1 16.8 %copy-start.3 = (bf16[2,2,128,128]{3,2,1,0:T(8,128)(2,1)S(1)}, bf16[2,2,128,128]{3,2,1,0:T(8,128)(2,1)}, u32[]{:S(2)}) copy-start(bf16[2,2,128,128]{3,2,1,0:T(8,128)(2,1)} %local_ref.3) | copy-start | bytes 393220
  3.1 16.8 %copy-start.6 = (bf16[128,64]{0,1:T(8,128)(2,1)S(1)}, bf16[128,64]{0,1:T(8,128)(2,1)}, u32[]{:S(2)}) copy-start(bf16[128,64]{0,1:T(8,128)(2,1)} %param.13) | copy-start | bytes 49156
  3.1 16.8 %copy-start.7 = (s32[1,16,16]{2,1,0:T(8,128)S(1)}, s32[1,16,16]{2,1,0:T(8,128)}, u32[]{:S(2)}) copy-start(s32[1,16,16]{2,1,0:T(8,128)} %rows_ref.1) | copy-start | bytes 3076
  3.2 16.8 %copy-start.8 = (s32[16,16]{1,0:T(8,128)S(1)}, s32[16,16]{1,0:T(8,128)}, u32[]{:S(2)}) copy-start(s32[16,16]{1,0:T(8,128)} %count_ref.1) | copy-start | bytes 3076
  3.2 16.8 %copy-start.10 = (s32[2,2]{1,0:T(2,128)S(1)}, s32[2,2]{1,0:T(2,128)}, u32[]{:S(2)}) copy-start(s32[2,2]{1,0:T(2,128)} %blocks_ref.3) | copy-start | bytes 52
  3.2 42.3 %all-to-all-start = ((bf16[16,32,512]{2,1,0:T(8,128)(2,1)}), bf16[16,32,512]{2,1,0:T(8,128)(2,1)S(1)}, u32[]{:S(2)}, u32[]{:S(2)}) async-start(bf16[16,32,512]{2,1,0:T(8,128)(2,1)} %shard_map.113), calls=%async_computation | async-start | bytes 1048576 | tf_op jit(solution)/shard_map/all_to_all | solution.py:351
  18.5 10.9 %copy-start.9 = (bf16[128,128]{1,0:T(8,128)(2,1)S(1)}, bf16[128,128]{1,0:T(8,128)(2,1)}, u32[]{:S(2)}) copy-start(bf16[128,128]{1,0:T(8,128)(2,1)} %conv_ref.1) | copy-start | bytes 98308
  18.6 10.9 %collective-permute-start = (bf16[256,512]{1,0:T(8,128)(2,1)S(1)}, bf16[256,512]{1,0:T(8,128)(2,1)S(1)}, u32[]{:S(2)}, u32[]{:S(2)}) collective-permute-start(bf16[256,512]{1,0:T(8,128)(2,1)S(1)} %copy-done.1), channel_id=1, source_target_pairs={{0,16},{1,17},{2,18},{3,19},{4,20},{5,21},{6,22},{7,23},{8,24},{9,... | collective-permute-start | bytes 786440 | tf_op jit(solution)/shard_map/ppermute | solution.py:352
  21.1 8.4 %copy-start.11 = (f32[128]{0:T(128)S(1)}, f32[128]{0:T(128)}, u32[]{:S(2)}) copy-start(f32[128]{0:T(128)} %param.12) | copy-start | bytes 1540
  31.0 0.8 %copy-start.4 = (f32[256,512]{1,0:T(8,128)}, f32[256,512]{1,0:T(8,128)S(1)}, u32[]{:S(2)}) copy-start(f32[256,512]{1,0:T(8,128)S(1)} %get-tuple-element.15.base_ref) | copy-start | bytes 1572868
  46.0 8.7 %copy-start.5 = (f32[256,512]{1,0:T(8,128)S(1)}, f32[256,512]{1,0:T(8,128)}, u32[]{:S(2)}) copy-start(f32[256,512]{1,0:T(8,128)} %copy-done.4) | copy-start | bytes 1572868

commit v4 on v3

--- a/solution.py
+++ b/solution.py
@@ -9,7 +9,8 @@
 PAIR = 2 * C
 F32 = jnp.float32
 BF16 = jnp.bfloat16
-FIRST = 12
+FIRST = 11
+ORDER = tuple((FIRST + (k + 1) // 2 * (1 if k % 2 else -1)) % 16 for k in range(16))
 
 
 def dot(a, b):
@@ -77,9 +78,13 @@
     return jnp.where(alive, values_ref[...].astype(F32), 0.0).astype(BF16)
 
 
-def turned(blocks, first):
-    first = first % blocks.shape[0]
-    return jnp.concatenate([blocks[first:], blocks[:first]], axis=0) if first else blocks
+def to_order(blocks):
+    return jnp.concatenate([blocks[q : q + 1] for q in ORDER], axis=0)
+
+
+def from_order(blocks):
+    places = [ORDER.index(q) for q in range(len(ORDER))]
+    return jnp.concatenate([blocks[k : k + 1] for k in places], axis=0)
 
 
 def tanh_sigmoid(preact):
@@ -143,10 +148,10 @@
     mix = two_steps(mix_ref[...])[:, PAIR:]
     mixed_grad = jnp.concatenate([dot(cot_ref[:, c], mix).astype(BF16) for c in pairs(columns)], axis=1)
     listed = dot_tn(pick, series_ref[...]).astype(BF16)
-    out_ref[0] = turned(listed.reshape(groups, cap, columns), FIRST)
+    out_ref[0] = to_order(listed.reshape(groups, cap, columns))
     sent[0].start()
     returned = dot_tn(live, mixed_grad).astype(BF16)
-    out_ref[1] = turned(returned.reshape(groups, cap, columns), FIRST)
+    out_ref[1] = to_order(returned.reshape(groups, cap, columns))
     sent[1].start()
     sent[0].wait()
     sent[1].wait()
@@ -225,7 +230,7 @@
     groups, both, columns = got_ref.shape
     cap = both // 2
     second_half = lax.axis_index("tm") >= lax.axis_size("tm") // 2
-    back = turned(got_ref[:, cap:, :], -FIRST).reshape(groups * cap, columns)
+    back = from_order(got_ref[:, cap:, :]).reshape(groups * cap, columns)
     upstream = (partial_ref[...] + dot(slots_ref[:, : groups * cap], back)).astype(BF16).astype(F32)
     for c, w in zip(pairs(columns), wides(columns)):
         up = upstream[:, c]
@@ -238,7 +243,7 @@
 
     @pl.when(jnp.logical_not(second_half))
     def _():
-        swap_ref[...] = turned(got_ref[:, :cap, :], -FIRST).reshape(groups * cap, columns)
+        swap_ref[...] = from_order(got_ref[:, :cap, :]).reshape(groups * cap, columns)
 
 
 def last_kernel(
@@ -269,7 +274,7 @@
     grad_copy = pltpu.make_async_copy(grad_ref, grad_hbm, gone.at[0])
     grad_copy.start()
     before = jnp.where(second_half, came, 0.0).astype(BF16)
-    listed = turned(got_ref[:, :cap, :], -FIRST).reshape(slots, columns)
+    listed = from_order(got_ref[:, :cap, :]).reshape(slots, columns)
     bias = bias_pair(bias_ref)
     kept = []
     for c in pairs(columns):
@@ -347,8 +352,7 @@
             pltpu.SemaphoreType.DMA((2,)),
         ],
     )
-    order = [(FIRST + k) % groups for k in range(groups)]
-    got = lax.all_to_all(send, "node", 0, 0, axis_index_groups=[order], tiled=True)
+    got = lax.all_to_all(send, "node", 0, 0, axis_index_groups=[list(ORDER)], tiled=True)
     delayed = lax.ppermute(series, "tm", [(i, i + half) for i in range(half)])
     partial, picked_live = call(
         local_grad_kernel,

time: 56.6 us -> 54.2 us (0.958)
  the two profiles are of different devices: /device:TPU:54 before, /device:TPU:60 now
where the time goes in v4:
time: 54.2 us; the launch traced here: 53.9 us
  waiting for transfers between devices  18.5 us (34%)
  starting transfers between devices  17.1 us (32%)
  blocking collectives  9.36 us (17%)
  Pallas kernels  7.29 us (13%)
  local copies, waits for them, and re-layouts  0.87 us (2%)
  between operations  0.82 us (2%)
    all_to_all x1, starting transfers between devices, local(): lax.all_to_all(send, 'node', 0, 0, axis_index_groups=[list(ORDER)], tiled...  15.8 us
    all_to_all x1, waiting for transfers between devices, local(): lax.all_to_all(send, 'node', 0, 0, axis_index_groups=[list(ORDER)], tiled...  10.1 us
    all_gather x1, blocking collectives, local(): lax.all_gather(swap, 'tm', axis_index_groups=[[i, i + half] for i in rang...  9.36 us
    ppermute x1, waiting for transfers between devices, local(): delayed = lax.ppermute(series, 'tm', [(i, i + half) for i in range(half)])  8.37 us
    pallas_call x5, Pallas kernels, call(): pl.pallas_call(kernel, out_shape=outs, in_specs=[SMEM if n in scalars els...  7.29 us
    ppermute x1, starting transfers between devices, local(): delayed = lax.ppermute(series, 'tm', [(i, i + half) for i in range(half)])  1.29 us
  transfers between devices with their start and end apart: 2, of which 2 were waited for; matrix products, arithmetic and copies ran while one was open for 0% of the time, Pallas kernels for 5%

profile of v4, /device:TPU:60, one launch (start us, length us, event | category | flops | bytes accessed | tf_op | source)
XLA Modules:
  0.0 53.9 jit_solution(698446977017404944)
XLA Ops:
  0.6 2.4 %shard_map.113 = bf16[16,32,512]{2,1,0:T(8,128)(2,1)} custom-call(s32[1,16,16]{2,1,0:T(8,128)} %rows_ref.1, bf16[256,512]{1,0:T(8,128)(2,1)} %series_ref.1, bf16[64,128]{1,0:T(8,128)(2,1)} %bitcast.4, bf16[256,512]{1,0:T(8,128)(2,1)} %cot_ref.3, s32[16,16]{1,0:T(8,128)} %count_ref.1, bf16[256,256]{1,0:T(8,128)(2,1)} %values_ref.1), custom_call_target="tpu_custom_call" | custom-call | flops 134217728 | bytes 2097152 | tf_op jit(solution)/shard_map/pallas_call | solution.py:306
  3.1 0.0 copy-start.1
  3.1 0.0 copy-start
  3.1 0.0 copy-start.2
  3.1 0.0 copy-start.3
  3.1 0.0 copy-start.6
  3.1 0.0 copy-start.7
  3.2 0.0 copy-start.8
  3.2 0.0 copy-start.10
  3.2 15.8 %all-to-all-start = ((bf16[16,32,512]{2,1,0:T(8,128)(2,1)}), bf16[16,32,512]{2,1,0:T(8,128)(2,1)S(1)}, u32[]{:S(2)}, u32[]{:S(2)}) async-start(bf16[16,32,512]{2,1,0:T(8,128)(2,1)} %shard_map.113), calls=%async_computation | async-start | bytes 1048576 | tf_op jit(solution)/shard_map/all_to_all | solution.py:355
  19.0 0.0 copy-done.1
  19.0 0.0 copy-start.9
  19.0 1.3 %collective-permute-start = (bf16[256,512]{1,0:T(8,128)(2,1)S(1)}, bf16[256,512]{1,0:T(8,128)(2,1)S(1)}, u32[]{:S(2)}, u32[]{:S(2)}) collective-permute-start(bf16[256,512]{1,0:T(8,128)(2,1)S(1)} %copy-done.1), channel_id=1, source_target_pairs={{0,16},{1,17},{2,18},{3,19},{4,20},{5,21},{6,22},{7,23},{8,24},{9,... | collective-permute-start | bytes 786440 | tf_op jit(solution)/shard_map/ppermute | solution.py:356
  20.3 0.0 copy-done
  20.4 0.0 copy-done.2
  20.4 0.0 copy-done.3
  20.4 0.0 copy-done.6
  20.4 0.0 copy-done.7
  20.4 0.0 copy-done.8
  20.4 0.0 copy-done.10
  20.4 1.1 %shard_map.114 = (f32[256,512]{1,0:T(8,128)S(1)}, bf16[256,512]{1,0:T(8,128)(2,1)S(1)}) custom-call(bf16[256,512]{1,0:T(8,128)(2,1)S(1)} %copy-done, bf16[64,128]{1,0:T(8,128)(2,1)S(1)} %bitcast.5, bf16[2,2,128,128]{3,2,1,0:T(8,128)(2,1)S(1)} %copy-done.3, s32[1,16,16]{2,1,0:T(8,128)S(1)} %copy-done.7, bf16[256,256]{1,0:T(8,128)(2,1)S(1)} %copy-done.2, ...), custom_call_target="tpu_custom_call" | custom-call | flops 134217728 | bytes 2097152 | tf_op jit(solution)/shard_map/pallas_call | solution.py:306
  21.6 0.0 copy-start.11
  21.6 8.4 %collective-permute-done.delayed_ref = bf16[256,512]{1,0:T(8,128)(2,1)S(1)} collective-permute-done((bf16[256,512]{1,0:T(8,128)(2,1)S(1)}, bf16[256,512]{1,0:T(8,128)(2,1)S(1)}, u32[]{:S(2)}, u32[]{:S(2)}) %collective-permute-start) | collective-permute-done | bytes 262176 | tf_op jit(solution)/shard_map/ppermute | solution.py:356
  30.0 0.0 copy-done.9
  30.0 0.0 copy-done.11
  30.0 1.5 %shard_map.115 = (f32[256,512]{1,0:T(8,128)S(1)}, f32[256,1024]{1,0:T(8,128)S(1)}, bf16[384,256]{1,0:T(8,128)(2,1)S(1)}) custom-call(bf16[256,512]{1,0:T(8,128)(2,1)S(1)} %copy-done.1, bf16[256,512]{1,0:T(8,128)(2,1)S(1)} %collective-permute-done.delayed_ref, bf16[128,128]{1,0:T(8,128)(2,1)S(1)} %copy-done.9, f32[1,128]{1,0:T(1,128)S(1)} %bitcast.7, ...), custom_call_target="tpu_custom_call" | custom-call | flops 134217728 | bytes 2097152 | tf_op jit(solution)/shard_map/pallas_call | solution.py:306
  31.5 0.0 copy-start.4
  31.5 0.8 %copy-done.4 = f32[256,512]{1,0:T(8,128)} copy-done((f32[256,512]{1,0:T(8,128)}, f32[256,512]{1,0:T(8,128)S(1)}, u32[]{:S(2)}) %copy-start.4) | copy-done | bytes 524312
  32.3 10.1 %all-to-all-done.got_ref = bf16[16,32,512]{2,1,0:T(8,128)(2,1)S(1)} async-done(((bf16[16,32,512]{2,1,0:T(8,128)(2,1)}), bf16[16,32,512]{2,1,0:T(8,128)(2,1)S(1)}, u32[]{:S(2)}, u32[]{:S(2)}) %all-to-all-start) | async-done | bytes 524320 | tf_op jit(solution)/shard_map/all_to_all | solution.py:355
  42.4 0.6 %shard_map.116 = (bf16[256,1024]{1,0:T(8,128)(2,1)S(1)}, bf16[256,512]{1,0:T(8,128)(2,1)S(1)}) custom-call(bf16[16,32,512]{2,1,0:T(8,128)(2,1)S(1)} %all-to-all-done.got_ref, f32[256,512]{1,0:T(8,128)S(1)} %get-tuple-element.9.partial_ref, f32[256,1024]{1,0:T(8,128)S(1)} %get-tuple-element.10.slope_ref, bf16[256,512]{1,0:T(8,128)(2,1)S(1)} %get-tuple-element.11.slots_ref, ...), custom_call_target="tpu_custom_call" | custom-call | flops 134217728 | bytes 2097152 | tf_op jit(solution)/shard_map/pallas_call | solution.py:306
  43.0 9.4 %all-gather = bf16[512,512]{1,0:T(8,128)(2,1)S(1)} all-gather(bf16[256,512]{1,0:T(8,128)(2,1)S(1)} %get-tuple-element.13), channel_id=2, replica_groups={{0,16},{1,17},{2,18},{3,19},{4,20},{5,21},{6,22},{7,23},{8,24},{9,25},{..., dimensions={0}, use_global_device_ids=true | all-gather | bytes 786432 | tf_op jit(solution)/shard_map/all_gather | solution.py:391
  52.3 1.6 %shard_map.117 = (bf16[256,512]{1,0:T(8,128)(2,1)}, bf16[256,512]{1,0:T(8,128)(2,1)}) custom-call(bf16[2,256,512]{2,1,0:T(8,128)(2,1)S(1)} %bitcast.3, bf16[16,32,512]{2,1,0:T(8,128)(2,1)S(1)} %all-to-all-done.got_ref, bf16[256,1024]{1,0:T(8,128)(2,1)S(1)} %get-tuple-element.14.gate_ref, bf16[256,512]{1,0:T(8,128)(2,1)S(1)} %get-tuple-element.11.slots_ref, ...), custom_call_target="tpu_custom_call" | custom-call | flops 134217728 | bytes 2097152 | tf_op jit(solution)/shard_map/pallas_call | solution.py:306
  (2 shorter events, 0.0 us)
Async XLA Ops:
  3.1 15.9 %copy-start.1 = (bf16[256,512]{1,0:T(8,128)(2,1)S(1)}, bf16[256,512]{1,0:T(8,128)(2,1)}, u32[]{:S(2)}) copy-start(bf16[256,512]{1,0:T(8,128)(2,1)} %series_ref.1) | copy-start | bytes 786436
  3.1 17.3 %copy-start = (bf16[256,512]{1,0:T(8,128)(2,1)S(1)}, bf16[256,512]{1,0:T(8,128)(2,1)}, u32[]{:S(2)}) copy-start(bf16[256,512]{1,0:T(8,128)(2,1)} %cot_ref.3) | copy-start | bytes 786436
  3.1 17.2 %copy-start.2 = (bf16[256,256]{1,0:T(8,128)(2,1)S(1)}, bf16[256,256]{1,0:T(8,128)(2,1)}, u32[]{:S(2)}) copy-start(bf16[256,256]{1,0:T(8,128)(2,1)} %values_ref.1) | copy-start | bytes 393220
  3.1 17.2 %copy-start.3 = (bf16[2,2,128,128]{3,2,1,0:T(8,128)(2,1)S(1)}, bf16[2,2,128,128]{3,2,1,0:T(8,128)(2,1)}, u32[]{:S(2)}) copy-start(bf16[2,2,128,128]{3,2,1,0:T(8,128)(2,1)} %local_ref.3) | copy-start | bytes 393220
  3.1 17.2 %copy-start.6 = (bf16[128,64]{0,1:T(8,128)(2,1)S(1)}, bf16[128,64]{0,1:T(8,128)(2,1)}, u32[]{:S(2)}) copy-start(bf16[128,64]{0,1:T(8,128)(2,1)} %param.13) | copy-start | bytes 49156
  3.1 17.2 %copy-start.7 = (s32[1,16,16]{2,1,0:T(8,128)S(1)}, s32[1,16,16]{2,1,0:T(8,128)}, u32[]{:S(2)}) copy-start(s32[1,16,16]{2,1,0:T(8,128)} %rows_ref.1) | copy-start | bytes 3076
  3.2 17.2 %copy-start.8 = (s32[16,16]{1,0:T(8,128)S(1)}, s32[16,16]{1,0:T(8,128)}, u32[]{:S(2)}) copy-start(s32[16,16]{1,0:T(8,128)} %count_ref.1) | copy-start | bytes 3076
  3.2 17.2 %copy-start.10 = (s32[2,2]{1,0:T(2,128)S(1)}, s32[2,2]{1,0:T(2,128)}, u32[]{:S(2)}) copy-start(s32[2,2]{1,0:T(2,128)} %blocks_ref.3) | copy-start | bytes 52
  3.2 39.2 %all-to-all-start = ((bf16[16,32,512]{2,1,0:T(8,128)(2,1)}), bf16[16,32,512]{2,1,0:T(8,128)(2,1)S(1)}, u32[]{:S(2)}, u32[]{:S(2)}) async-start(bf16[16,32,512]{2,1,0:T(8,128)(2,1)} %shard_map.113), calls=%async_computation | async-start | bytes 1048576 | tf_op jit(solution)/shard_map/all_to_all | solution.py:355
  19.0 10.9 %copy-start.9 = (bf16[128,128]{1,0:T(8,128)(2,1)S(1)}, bf16[128,128]{1,0:T(8,128)(2,1)}, u32[]{:S(2)}) copy-start(bf16[128,128]{1,0:T(8,128)(2,1)} %conv_ref.1) | copy-start | bytes 98308
  19.0 10.9 %collective-permute-start = (bf16[256,512]{1,0:T(8,128)(2,1)S(1)}, bf16[256,512]{1,0:T(8,128)(2,1)S(1)}, u32[]{:S(2)}, u32[]{:S(2)}) collective-permute-start(bf16[256,512]{1,0:T(8,128)(2,1)S(1)} %copy-done.1), channel_id=1, source_target_pairs={{0,16},{1,17},{2,18},{3,19},{4,20},{5,21},{6,22},{7,23},{8,24},{9,... | collective-permute-start | bytes 786440 | tf_op jit(solution)/shard_map/ppermute | solution.py:356
  21.6 8.4 %copy-start.11 = (f32[128]{0:T(128)S(1)}, f32[128]{0:T(128)}, u32[]{:S(2)}) copy-start(f32[128]{0:T(128)} %param.12) | copy-start | bytes 1540
  31.5 0.8 %copy-start.4 = (f32[256,512]{1,0:T(8,128)}, f32[256,512]{1,0:T(8,128)S(1)}, u32[]{:S(2)}) copy-start(f32[256,512]{1,0:T(8,128)S(1)} %get-tuple-element.15.base_ref) | copy-start | bytes 1572868
  43.0 9.4 %copy-start.5 = (f32[256,512]{1,0:T(8,128)S(1)}, f32[256,512]{1,0:T(8,128)}, u32[]{:S(2)}) copy-start(f32[256,512]{1,0:T(8,128)} %copy-done.4) | copy-start | bytes 1572868

commit v5 on v4

--- a/solution.py
+++ b/solution.py
@@ -9,8 +9,7 @@
 PAIR = 2 * C
 F32 = jnp.float32
 BF16 = jnp.bfloat16
-FIRST = 11
-ORDER = tuple((FIRST + (k + 1) // 2 * (1 if k % 2 else -1)) % 16 for k in range(16))
+ORDER = (11, 12, 6, 13, 9, 14, 8, 15, 7, 0, 10, 1, 5, 2, 4, 3)
 
 
 def dot(a, b):
@@ -267,12 +266,6 @@
     nodes = cot_ref.shape[0]
     second_half = lax.axis_index("tm") >= lax.axis_size("tm") // 2
     came = came_ref[jnp.where(second_half, 0, 1)].astype(F32)
-    later = jnp.where(second_half, 0.0, came)
-    for c, w in zip(pairs(columns), wides(columns)):
-        grad = (dot_nt(gate_ref[:, w], weight_ref[PAIR : 2 * PAIR]) + later[:, c]).astype(BF16)
-        grad_ref[:, c] = (cot_ref[:, c].astype(F32) + grad.astype(F32)).astype(BF16)
-    grad_copy = pltpu.make_async_copy(grad_ref, grad_hbm, gone.at[0])
-    grad_copy.start()
     before = jnp.where(second_half, came, 0.0).astype(BF16)
     listed = from_order(got_ref[:, :cap, :]).reshape(slots, columns)
     bias = bias_pair(bias_ref)
@@ -282,18 +275,20 @@
         filtered, opened = tanh_sigmoid(dot(stacked, weight_ref[: 2 * PAIR]) + bias)
         kept.append((filtered * opened).astype(BF16))
     hidden = jnp.concatenate(kept, axis=1)
-    copies = []
-    for n in range(2):
-        rows = pl.ds(n * (nodes // 2), nodes // 2)
-        mixed = dot(slots_ref[rows, slots:], hidden).astype(BF16)
-        for c in pairs(columns):
-            added = dot_nt(mixed[:, c], weight_ref[2 * PAIR :, PAIR:])
-            out_ref[rows, c] = (base_ref[rows, c] + added).astype(BF16)
-        copies.append(pltpu.make_async_copy(out_ref.at[rows], out_hbm.at[rows], gone.at[n + 1]))
-        copies[n].start()
+    mixed = dot(slots_ref[:, slots:], hidden).astype(BF16)
+    for c in pairs(columns):
+        added = dot_nt(mixed[:, c], weight_ref[2 * PAIR :, PAIR:])
+        out_ref[:, c] = (base_ref[:, c] + added).astype(BF16)
+    out_copy = pltpu.make_async_copy(out_ref, out_hbm, gone.at[0])
+    out_copy.start()
+    later = jnp.where(second_half, 0.0, came)
+    for c, w in zip(pairs(columns), wides(columns)):
+        grad = (dot_nt(gate_ref[:, w], weight_ref[PAIR : 2 * PAIR]) + later[:, c]).astype(BF16)
+        grad_ref[:, c] = (cot_ref[:, c].astype(F32) + grad.astype(F32)).astype(BF16)
+    grad_copy = pltpu.make_async_copy(grad_ref, grad_hbm, gone.at[1])
+    grad_copy.start()
+    out_copy.wait()
     grad_copy.wait()
-    for copy in copies:
-        copy.wait()
 
 
 VMEM = pl.BlockSpec(memory_space=pltpu.VMEM)
@@ -404,7 +399,7 @@
         scratch=[
             pltpu.VMEM((nodes, columns), BF16),
             pltpu.VMEM((nodes, columns), BF16),
-            pltpu.SemaphoreType.DMA((3,)),
+            pltpu.SemaphoreType.DMA((2,)),
         ],
     )
 

time: 54.2 us -> 53.9 us (level)
  the two profiles are of different devices: /device:TPU:60 before, /device:TPU:26 now
where the time goes in v5:
time: 53.9 us; the launch traced here: 53.6 us
  waiting for transfers between devices  18.4 us (34%)
  starting transfers between devices  17.6 us (33%)
  blocking collectives  8.68 us (16%)
  Pallas kernels  7.18 us (13%)
  local copies, waits for them, and re-layouts  0.87 us (2%)
  between operations  0.82 us (2%)
    all_to_all x1, starting transfers between devices, local(): lax.all_to_all(send, 'node', 0, 0, axis_index_groups=[list(ORDER)], tiled...  16.3 us
    all_to_all x1, waiting for transfers between devices, local(): lax.all_to_all(send, 'node', 0, 0, axis_index_groups=[list(ORDER)], tiled...  10.1 us
    all_gather x1, blocking collectives, local(): lax.all_gather(swap, 'tm', axis_index_groups=[[i, i + half] for i in rang...  8.68 us
    ppermute x1, waiting for transfers between devices, local(): delayed = lax.ppermute(series, 'tm', [(i, i + half) for i in range(half)])  8.36 us
    pallas_call x5, Pallas kernels, call(): pl.pallas_call(kernel, out_shape=outs, in_specs=[SMEM if n in scalars els...  7.18 us
    ppermute x1, starting transfers between devices, local(): delayed = lax.ppermute(series, 'tm', [(i, i + half) for i in range(half)])  1.29 us
  transfers between devices with their start and end apart: 2, of which 2 were waited for; matrix products, arithmetic and copies ran while one was open for 0% of the time, Pallas kernels for 5%

profile of v5, /device:TPU:26, one launch (start us, length us, event | category | flops | bytes accessed | tf_op | source)
XLA Modules:
  0.0 53.6 jit_solution(3172918895681259865)
XLA Ops:
  0.6 2.4 %shard_map.113 = bf16[16,32,512]{2,1,0:T(8,128)(2,1)} custom-call(s32[1,16,16]{2,1,0:T(8,128)} %rows_ref.1, bf16[256,512]{1,0:T(8,128)(2,1)} %series_ref.1, bf16[64,128]{1,0:T(8,128)(2,1)} %bitcast.4, bf16[256,512]{1,0:T(8,128)(2,1)} %cot_ref.3, s32[16,16]{1,0:T(8,128)} %count_ref.1, bf16[256,256]{1,0:T(8,128)(2,1)} %values_ref.1), custom_call_target="tpu_custom_call" | custom-call | flops 134217728 | bytes 2097152 | tf_op jit(solution)/shard_map/pallas_call | solution.py:301
  3.1 0.0 copy-start.1
  3.1 0.0 copy-start
  3.1 0.0 copy-start.2
  3.1 0.0 copy-start.3
  3.1 0.0 copy-start.6
  3.1 0.0 copy-start.7
  3.2 0.0 copy-start.8
  3.2 0.0 copy-start.10
  3.2 16.3 %all-to-all-start = ((bf16[16,32,512]{2,1,0:T(8,128)(2,1)}), bf16[16,32,512]{2,1,0:T(8,128)(2,1)S(1)}, u32[]{:S(2)}, u32[]{:S(2)}) async-start(bf16[16,32,512]{2,1,0:T(8,128)(2,1)} %shard_map.113), calls=%async_computation | async-start | bytes 1048576 | tf_op jit(solution)/shard_map/all_to_all | solution.py:350
  19.5 0.0 copy-done.1
  19.5 0.0 copy-start.9
  19.5 1.3 %collective-permute-start = (bf16[256,512]{1,0:T(8,128)(2,1)S(1)}, bf16[256,512]{1,0:T(8,128)(2,1)S(1)}, u32[]{:S(2)}, u32[]{:S(2)}) collective-permute-start(bf16[256,512]{1,0:T(8,128)(2,1)S(1)} %copy-done.1), channel_id=1, source_target_pairs={{0,16},{1,17},{2,18},{3,19},{4,20},{5,21},{6,22},{7,23},{8,24},{9,... | collective-permute-start | bytes 786440 | tf_op jit(solution)/shard_map/ppermute | solution.py:351
  20.8 0.0 copy-done
  20.8 0.0 copy-done.2
  20.8 0.0 copy-done.3
  20.8 0.0 copy-done.6
  20.8 0.0 copy-done.7
  20.8 0.0 copy-done.8
  20.9 0.0 copy-done.10
  20.9 1.1 %shard_map.114 = (f32[256,512]{1,0:T(8,128)S(1)}, bf16[256,512]{1,0:T(8,128)(2,1)S(1)}) custom-call(bf16[256,512]{1,0:T(8,128)(2,1)S(1)} %copy-done, bf16[64,128]{1,0:T(8,128)(2,1)S(1)} %bitcast.5, bf16[2,2,128,128]{3,2,1,0:T(8,128)(2,1)S(1)} %copy-done.3, s32[1,16,16]{2,1,0:T(8,128)S(1)} %copy-done.7, bf16[256,256]{1,0:T(8,128)(2,1)S(1)} %copy-done.2, ...), custom_call_target="tpu_custom_call" | custom-call | flops 134217728 | bytes 2097152 | tf_op jit(solution)/shard_map/pallas_call | solution.py:301
  22.0 0.0 copy-start.11
  22.0 8.4 %collective-permute-done.delayed_ref = bf16[256,512]{1,0:T(8,128)(2,1)S(1)} collective-permute-done((bf16[256,512]{1,0:T(8,128)(2,1)S(1)}, bf16[256,512]{1,0:T(8,128)(2,1)S(1)}, u32[]{:S(2)}, u32[]{:S(2)}) %collective-permute-start) | collective-permute-done | bytes 262176 | tf_op jit(solution)/shard_map/ppermute | solution.py:351
  30.4 0.0 copy-done.9
  30.4 0.0 copy-done.11
  30.4 1.5 %shard_map.115 = (f32[256,512]{1,0:T(8,128)S(1)}, f32[256,1024]{1,0:T(8,128)S(1)}, bf16[384,256]{1,0:T(8,128)(2,1)S(1)}) custom-call(bf16[256,512]{1,0:T(8,128)(2,1)S(1)} %copy-done.1, bf16[256,512]{1,0:T(8,128)(2,1)S(1)} %collective-permute-done.delayed_ref, bf16[128,128]{1,0:T(8,128)(2,1)S(1)} %copy-done.9, f32[1,128]{1,0:T(1,128)S(1)} %bitcast.7, ...), custom_call_target="tpu_custom_call" | custom-call | flops 134217728 | bytes 2097152 | tf_op jit(solution)/shard_map/pallas_call | solution.py:301
  32.0 0.0 copy-start.4
  32.0 0.8 %copy-done.4 = f32[256,512]{1,0:T(8,128)} copy-done((f32[256,512]{1,0:T(8,128)}, f32[256,512]{1,0:T(8,128)S(1)}, u32[]{:S(2)}) %copy-start.4) | copy-done | bytes 524312
  32.8 10.1 %all-to-all-done.got_ref = bf16[16,32,512]{2,1,0:T(8,128)(2,1)S(1)} async-done(((bf16[16,32,512]{2,1,0:T(8,128)(2,1)}), bf16[16,32,512]{2,1,0:T(8,128)(2,1)S(1)}, u32[]{:S(2)}, u32[]{:S(2)}) %all-to-all-start) | async-done | bytes 524320 | tf_op jit(solution)/shard_map/all_to_all | solution.py:350
  42.8 0.6 %shard_map.116 = (bf16[256,1024]{1,0:T(8,128)(2,1)S(1)}, bf16[256,512]{1,0:T(8,128)(2,1)S(1)}) custom-call(bf16[16,32,512]{2,1,0:T(8,128)(2,1)S(1)} %all-to-all-done.got_ref, f32[256,512]{1,0:T(8,128)S(1)} %get-tuple-element.9.partial_ref, f32[256,1024]{1,0:T(8,128)S(1)} %get-tuple-element.10.slope_ref, bf16[256,512]{1,0:T(8,128)(2,1)S(1)} %get-tuple-element.11.slots_ref, ...), custom_call_target="tpu_custom_call" | custom-call | flops 134217728 | bytes 2097152 | tf_op jit(solution)/shard_map/pallas_call | solution.py:301
  43.4 8.7 %all-gather = bf16[512,512]{1,0:T(8,128)(2,1)S(1)} all-gather(bf16[256,512]{1,0:T(8,128)(2,1)S(1)} %get-tuple-element.13), channel_id=2, replica_groups={{0,16},{1,17},{2,18},{3,19},{4,20},{5,21},{6,22},{7,23},{8,24},{9,25},{..., dimensions={0}, use_global_device_ids=true | all-gather | bytes 786432 | tf_op jit(solution)/shard_map/all_gather | solution.py:386
  52.1 1.5 %shard_map.117 = (bf16[256,512]{1,0:T(8,128)(2,1)}, bf16[256,512]{1,0:T(8,128)(2,1)}) custom-call(bf16[2,256,512]{2,1,0:T(8,128)(2,1)S(1)} %bitcast.3, bf16[16,32,512]{2,1,0:T(8,128)(2,1)S(1)} %all-to-all-done.got_ref, bf16[256,1024]{1,0:T(8,128)(2,1)S(1)} %get-tuple-element.14.gate_ref, bf16[256,512]{1,0:T(8,128)(2,1)S(1)} %get-tuple-element.11.slots_ref, ...), custom_call_target="tpu_custom_call" | custom-call | flops 134217728 | bytes 2097152 | tf_op jit(solution)/shard_map/pallas_call | solution.py:301
  (2 shorter events, 0.0 us)
Async XLA Ops:
  3.1 16.4 %copy-start.1 = (bf16[256,512]{1,0:T(8,128)(2,1)S(1)}, bf16[256,512]{1,0:T(8,128)(2,1)}, u32[]{:S(2)}) copy-start(bf16[256,512]{1,0:T(8,128)(2,1)} %series_ref.1) | copy-start | bytes 786436
  3.1 17.7 %copy-start = (bf16[256,512]{1,0:T(8,128)(2,1)S(1)}, bf16[256,512]{1,0:T(8,128)(2,1)}, u32[]{:S(2)}) copy-start(bf16[256,512]{1,0:T(8,128)(2,1)} %cot_ref.3) | copy-start | bytes 786436
  3.1 17.7 %copy-start.2 = (bf16[256,256]{1,0:T(8,128)(2,1)S(1)}, bf16[256,256]{1,0:T(8,128)(2,1)}, u32[]{:S(2)}) copy-start(bf16[256,256]{1,0:T(8,128)(2,1)} %values_ref.1) | copy-start | bytes 393220
  3.1 17.7 %copy-start.3 = (bf16[2,2,128,128]{3,2,1,0:T(8,128)(2,1)S(1)}, bf16[2,2,128,128]{3,2,1,0:T(8,128)(2,1)}, u32[]{:S(2)}) copy-start(bf16[2,2,128,128]{3,2,1,0:T(8,128)(2,1)} %local_ref.3) | copy-start | bytes 393220
  3.1 17.7 %copy-start.6 = (bf16[128,64]{0,1:T(8,128)(2,1)S(1)}, bf16[128,64]{0,1:T(8,128)(2,1)}, u32[]{:S(2)}) copy-start(bf16[128,64]{0,1:T(8,128)(2,1)} %param.13) | copy-start | bytes 49156
  3.1 17.7 %copy-start.7 = (s32[1,16,16]{2,1,0:T(8,128)S(1)}, s32[1,16,16]{2,1,0:T(8,128)}, u32[]{:S(2)}) copy-start(s32[1,16,16]{2,1,0:T(8,128)} %rows_ref.1) | copy-start | bytes 3076
  3.2 17.7 %copy-start.8 = (s32[16,16]{1,0:T(8,128)S(1)}, s32[16,16]{1,0:T(8,128)}, u32[]{:S(2)}) copy-start(s32[16,16]{1,0:T(8,128)} %count_ref.1) | copy-start | bytes 3076
  3.2 17.7 %copy-start.10 = (s32[2,2]{1,0:T(2,128)S(1)}, s32[2,2]{1,0:T(2,128)}, u32[]{:S(2)}) copy-start(s32[2,2]{1,0:T(2,128)} %blocks_ref.3) | copy-start | bytes 52
  3.2 39.7 %all-to-all-start = ((bf16[16,32,512]{2,1,0:T(8,128)(2,1)}), bf16[16,32,512]{2,1,0:T(8,128)(2,1)S(1)}, u32[]{:S(2)}, u32[]{:S(2)}) async-start(bf16[16,32,512]{2,1,0:T(8,128)(2,1)} %shard_map.113), calls=%async_computation | async-start | bytes 1048576 | tf_op jit(solution)/shard_map/all_to_all | solution.py:350
  19.5 10.9 %copy-start.9 = (bf16[128,128]{1,0:T(8,128)(2,1)S(1)}, bf16[128,128]{1,0:T(8,128)(2,1)}, u32[]{:S(2)}) copy-start(bf16[128,128]{1,0:T(8,128)(2,1)} %conv_ref.1) | copy-start | bytes 98308
  19.5 10.9 %collective-permute-start = (bf16[256,512]{1,0:T(8,128)(2,1)S(1)}, bf16[256,512]{1,0:T(8,128)(2,1)S(1)}, u32[]{:S(2)}, u32[]{:S(2)}) collective-permute-start(bf16[256,512]{1,0:T(8,128)(2,1)S(1)} %copy-done.1), channel_id=1, source_target_pairs={{0,16},{1,17},{2,18},{3,19},{4,20},{5,21},{6,22},{7,23},{8,24},{9,... | collective-permute-start | bytes 786440 | tf_op jit(solution)/shard_map/ppermute | solution.py:351
  22.0 8.4 %copy-start.11 = (f32[128]{0:T(128)S(1)}, f32[128]{0:T(128)}, u32[]{:S(2)}) copy-start(f32[128]{0:T(128)} %param.12) | copy-start | bytes 1540
  32.0 0.8 %copy-start.4 = (f32[256,512]{1,0:T(8,128)}, f32[256,512]{1,0:T(8,128)S(1)}, u32[]{:S(2)}) copy-start(f32[256,512]{1,0:T(8,128)S(1)} %get-tuple-element.15.base_ref) | copy-start | bytes 1572868
  43.4 8.7 %copy-start.5 = (f32[256,512]{1,0:T(8,128)S(1)}, f32[256,512]{1,0:T(8,128)}, u32[]{:S(2)}) copy-start(f32[256,512]{1,0:T(8,128)} %copy-done.4) | copy-start | bytes 1572868

commit v6 on v5

--- a/solution.py
+++ b/solution.py
@@ -140,11 +140,13 @@
         pltpu.make_async_copy(out_ref.at[n], out_hbm.at[:, pl.ds(n * cap, cap), :], gone.at[n])
         for n in range(2)
     ]
-    for copy in brought:
-        copy.wait()
+    for n in (0, 4, 2):
+        brought[n].wait()
+    mix = two_steps(mix_ref[...])[:, PAIR:]
     pick = picker(rows_ref, nodes, slots)
+    for n in (1, 3, 5):
+        brought[n].wait()
     live = live_values(values_ref, count_ref)
-    mix = two_steps(mix_ref[...])[:, PAIR:]
     mixed_grad = jnp.concatenate([dot(cot_ref[:, c], mix).astype(BF16) for c in pairs(columns)], axis=1)
     listed = dot_tn(pick, series_ref[...]).astype(BF16)
     out_ref[0] = to_order(listed.reshape(groups, cap, columns))

time: 53.9 us -> 53.8 us (level)
  no operation moved by 1% of the time
where the time goes in v6:
time: 53.8 us; the launch traced here: 53.4 us
  waiting for transfers between devices  18.4 us (34%)
  starting transfers between devices  17.6 us (33%)
  blocking collectives  8.68 us (16%)
  Pallas kernels  7.05 us (13%)
  local copies, waits for them, and re-layouts  0.87 us (2%)
  between operations  0.82 us (2%)
    all_to_all x1, starting transfers between devices, local(): lax.all_to_all(send, 'node', 0, 0, axis_index_groups=[list(ORDER)], tiled...  16.3 us
    all_to_all x1, waiting for transfers between devices, local(): lax.all_to_all(send, 'node', 0, 0, axis_index_groups=[list(ORDER)], tiled...  10.1 us
    all_gather x1, blocking collectives, local(): lax.all_gather(swap, 'tm', axis_index_groups=[[i, i + half] for i in rang...  8.68 us
    ppermute x1, waiting for transfers between devices, local(): delayed = lax.ppermute(series, 'tm', [(i, i + half) for i in range(half)])  8.36 us
    pallas_call x5, Pallas kernels, call(): pl.pallas_call(kernel, out_shape=outs, in_specs=[SMEM if n in scalars els...  7.05 us
    ppermute x1, starting transfers between devices, local(): delayed = lax.ppermute(series, 'tm', [(i, i + half) for i in range(half)])  1.29 us
  transfers between devices with their start and end apart: 2, of which 2 were waited for; matrix products, arithmetic and copies ran while one was open for 0% of the time, Pallas kernels for 5%

profile of v6, /device:TPU:26, one launch (start us, length us, event | category | flops | bytes accessed | tf_op | source)
XLA Modules:
  0.0 53.4 jit_solution(14325250222826952265)
XLA Ops:
  0.6 2.3 %shard_map.113 = bf16[16,32,512]{2,1,0:T(8,128)(2,1)} custom-call(s32[1,16,16]{2,1,0:T(8,128)} %rows_ref.1, bf16[256,512]{1,0:T(8,128)(2,1)} %series_ref.1, bf16[64,128]{1,0:T(8,128)(2,1)} %bitcast.4, bf16[256,512]{1,0:T(8,128)(2,1)} %cot_ref.3, s32[16,16]{1,0:T(8,128)} %count_ref.1, bf16[256,256]{1,0:T(8,128)(2,1)} %values_ref.1), custom_call_target="tpu_custom_call" | custom-call | flops 134217728 | bytes 2097152 | tf_op jit(solution)/shard_map/pallas_call | solution.py:303
  3.0 0.0 copy-start.1
  3.0 0.0 copy-start
  3.0 0.0 copy-start.2
  3.0 0.0 copy-start.3
  3.0 0.0 copy-start.6
  3.0 0.0 copy-start.7
  3.0 0.0 copy-start.8
  3.0 0.0 copy-start.10
  3.0 16.3 %all-to-all-start = ((bf16[16,32,512]{2,1,0:T(8,128)(2,1)}), bf16[16,32,512]{2,1,0:T(8,128)(2,1)S(1)}, u32[]{:S(2)}, u32[]{:S(2)}) async-start(bf16[16,32,512]{2,1,0:T(8,128)(2,1)} %shard_map.113), calls=%async_computation | async-start | bytes 1048576 | tf_op jit(solution)/shard_map/all_to_all | solution.py:352
  19.3 0.0 copy-done.1
  19.3 0.0 copy-start.9
  19.4 1.3 %collective-permute-start = (bf16[256,512]{1,0:T(8,128)(2,1)S(1)}, bf16[256,512]{1,0:T(8,128)(2,1)S(1)}, u32[]{:S(2)}, u32[]{:S(2)}) collective-permute-start(bf16[256,512]{1,0:T(8,128)(2,1)S(1)} %copy-done.1), channel_id=1, source_target_pairs={{0,16},{1,17},{2,18},{3,19},{4,20},{5,21},{6,22},{7,23},{8,24},{9,... | collective-permute-start | bytes 786440 | tf_op jit(solution)/shard_map/ppermute | solution.py:353
  20.7 0.0 copy-done
  20.7 0.0 copy-done.2
  20.7 0.0 copy-done.3
  20.7 0.0 copy-done.6
  20.7 0.0 copy-done.7
  20.7 0.0 copy-done.8
  20.7 0.0 copy-done.10
  20.7 1.1 %shard_map.114 = (f32[256,512]{1,0:T(8,128)S(1)}, bf16[256,512]{1,0:T(8,128)(2,1)S(1)}) custom-call(bf16[256,512]{1,0:T(8,128)(2,1)S(1)} %copy-done, bf16[64,128]{1,0:T(8,128)(2,1)S(1)} %bitcast.5, bf16[2,2,128,128]{3,2,1,0:T(8,128)(2,1)S(1)} %copy-done.3, s32[1,16,16]{2,1,0:T(8,128)S(1)} %copy-done.7, bf16[256,256]{1,0:T(8,128)(2,1)S(1)} %copy-done.2, ...), custom_call_target="tpu_custom_call" | custom-call | flops 134217728 | bytes 2097152 | tf_op jit(solution)/shard_map/pallas_call | solution.py:303
  21.9 0.0 copy-start.11
  21.9 8.4 %collective-permute-done.delayed_ref = bf16[256,512]{1,0:T(8,128)(2,1)S(1)} collective-permute-done((bf16[256,512]{1,0:T(8,128)(2,1)S(1)}, bf16[256,512]{1,0:T(8,128)(2,1)S(1)}, u32[]{:S(2)}, u32[]{:S(2)}) %collective-permute-start) | collective-permute-done | bytes 262176 | tf_op jit(solution)/shard_map/ppermute | solution.py:353
  30.3 0.0 copy-done.9
  30.3 0.0 copy-done.11
  30.3 1.5 %shard_map.115 = (f32[256,512]{1,0:T(8,128)S(1)}, f32[256,1024]{1,0:T(8,128)S(1)}, bf16[384,256]{1,0:T(8,128)(2,1)S(1)}) custom-call(bf16[256,512]{1,0:T(8,128)(2,1)S(1)} %copy-done.1, bf16[256,512]{1,0:T(8,128)(2,1)S(1)} %collective-permute-done.delayed_ref, bf16[128,128]{1,0:T(8,128)(2,1)S(1)} %copy-done.9, f32[1,128]{1,0:T(1,128)S(1)} %bitcast.7, ...), custom_call_target="tpu_custom_call" | custom-call | flops 134217728 | bytes 2097152 | tf_op jit(solution)/shard_map/pallas_call | solution.py:303
  31.8 0.0 copy-start.4
  31.8 0.8 %copy-done.4 = f32[256,512]{1,0:T(8,128)} copy-done((f32[256,512]{1,0:T(8,128)}, f32[256,512]{1,0:T(8,128)S(1)}, u32[]{:S(2)}) %copy-start.4) | copy-done | bytes 524312
  32.6 10.1 %all-to-all-done.got_ref = bf16[16,32,512]{2,1,0:T(8,128)(2,1)S(1)} async-done(((bf16[16,32,512]{2,1,0:T(8,128)(2,1)}), bf16[16,32,512]{2,1,0:T(8,128)(2,1)S(1)}, u32[]{:S(2)}, u32[]{:S(2)}) %all-to-all-start) | async-done | bytes 524320 | tf_op jit(solution)/shard_map/all_to_all | solution.py:352
  42.7 0.6 %shard_map.116 = (bf16[256,1024]{1,0:T(8,128)(2,1)S(1)}, bf16[256,512]{1,0:T(8,128)(2,1)S(1)}) custom-call(bf16[16,32,512]{2,1,0:T(8,128)(2,1)S(1)} %all-to-all-done.got_ref, f32[256,512]{1,0:T(8,128)S(1)} %get-tuple-element.9.partial_ref, f32[256,1024]{1,0:T(8,128)S(1)} %get-tuple-element.10.slope_ref, bf16[256,512]{1,0:T(8,128)(2,1)S(1)} %get-tuple-element.11.slots_ref, ...), custom_call_target="tpu_custom_call" | custom-call | flops 134217728 | bytes 2097152 | tf_op jit(solution)/shard_map/pallas_call | solution.py:303
  43.3 8.7 %all-gather = bf16[512,512]{1,0:T(8,128)(2,1)S(1)} all-gather(bf16[256,512]{1,0:T(8,128)(2,1)S(1)} %get-tuple-element.13), channel_id=2, replica_groups={{0,16},{1,17},{2,18},{3,19},{4,20},{5,21},{6,22},{7,23},{8,24},{9,25},{..., dimensions={0}, use_global_device_ids=true | all-gather | bytes 786432 | tf_op jit(solution)/shard_map/all_gather | solution.py:388
  52.0 1.5 %shard_map.117 = (bf16[256,512]{1,0:T(8,128)(2,1)}, bf16[256,512]{1,0:T(8,128)(2,1)}) custom-call(bf16[2,256,512]{2,1,0:T(8,128)(2,1)S(1)} %bitcast.3, bf16[16,32,512]{2,1,0:T(8,128)(2,1)S(1)} %all-to-all-done.got_ref, bf16[256,1024]{1,0:T(8,128)(2,1)S(1)} %get-tuple-element.14.gate_ref, bf16[256,512]{1,0:T(8,128)(2,1)S(1)} %get-tuple-element.11.slots_ref, ...), custom_call_target="tpu_custom_call" | custom-call | flops 134217728 | bytes 2097152 | tf_op jit(solution)/shard_map/pallas_call | solution.py:303
  (2 shorter events, 0.0 us)
Async XLA Ops:
  3.0 16.4 %copy-start.1 = (bf16[256,512]{1,0:T(8,128)(2,1)S(1)}, bf16[256,512]{1,0:T(8,128)(2,1)}, u32[]{:S(2)}) copy-start(bf16[256,512]{1,0:T(8,128)(2,1)} %series_ref.1) | copy-start | bytes 786436
  3.0 17.7 %copy-start = (bf16[256,512]{1,0:T(8,128)(2,1)S(1)}, bf16[256,512]{1,0:T(8,128)(2,1)}, u32[]{:S(2)}) copy-start(bf16[256,512]{1,0:T(8,128)(2,1)} %cot_ref.3) | copy-start | bytes 786436
  3.0 17.7 %copy-start.2 = (bf16[256,256]{1,0:T(8,128)(2,1)S(1)}, bf16[256,256]{1,0:T(8,128)(2,1)}, u32[]{:S(2)}) copy-start(bf16[256,256]{1,0:T(8,128)(2,1)} %values_ref.1) | copy-start | bytes 393220
  3.0 17.7 %copy-start.3 = (bf16[2,2,128,128]{3,2,1,0:T(8,128)(2,1)S(1)}, bf16[2,2,128,128]{3,2,1,0:T(8,128)(2,1)}, u32[]{:S(2)}) copy-start(bf16[2,2,128,128]{3,2,1,0:T(8,128)(2,1)} %local_ref.3) | copy-start | bytes 393220
  3.0 17.7 %copy-start.6 = (bf16[128,64]{0,1:T(8,128)(2,1)S(1)}, bf16[128,64]{0,1:T(8,128)(2,1)}, u32[]{:S(2)}) copy-start(bf16[128,64]{0,1:T(8,128)(2,1)} %param.13) | copy-start | bytes 49156
  3.0 17.7 %copy-start.7 = (s32[1,16,16]{2,1,0:T(8,128)S(1)}, s32[1,16,16]{2,1,0:T(8,128)}, u32[]{:S(2)}) copy-start(s32[1,16,16]{2,1,0:T(8,128)} %rows_ref.1) | copy-start | bytes 3076
  3.0 17.7 %copy-start.8 = (s32[16,16]{1,0:T(8,128)S(1)}, s32[16,16]{1,0:T(8,128)}, u32[]{:S(2)}) copy-start(s32[16,16]{1,0:T(8,128)} %count_ref.1) | copy-start | bytes 3076
  3.0 17.7 %copy-start.10 = (s32[2,2]{1,0:T(2,128)S(1)}, s32[2,2]{1,0:T(2,128)}, u32[]{:S(2)}) copy-start(s32[2,2]{1,0:T(2,128)} %blocks_ref.3) | copy-start | bytes 52
  3.0 39.7 %all-to-all-start = ((bf16[16,32,512]{2,1,0:T(8,128)(2,1)}), bf16[16,32,512]{2,1,0:T(8,128)(2,1)S(1)}, u32[]{:S(2)}, u32[]{:S(2)}) async-start(bf16[16,32,512]{2,1,0:T(8,128)(2,1)} %shard_map.113), calls=%async_computation | async-start | bytes 1048576 | tf_op jit(solution)/shard_map/all_to_all | solution.py:352
  19.3 10.9 %copy-start.9 = (bf16[128,128]{1,0:T(8,128)(2,1)S(1)}, bf16[128,128]{1,0:T(8,128)(2,1)}, u32[]{:S(2)}) copy-start(bf16[128,128]{1,0:T(8,128)(2,1)} %conv_ref.1) | copy-start | bytes 98308
  19.4 10.9 %collective-permute-start = (bf16[256,512]{1,0:T(8,128)(2,1)S(1)}, bf16[256,512]{1,0:T(8,128)(2,1)S(1)}, u32[]{:S(2)}, u32[]{:S(2)}) collective-permute-start(bf16[256,512]{1,0:T(8,128)(2,1)S(1)} %copy-done.1), channel_id=1, source_target_pairs={{0,16},{1,17},{2,18},{3,19},{4,20},{5,21},{6,22},{7,23},{8,24},{9,... | collective-permute-start | bytes 786440 | tf_op jit(solution)/shard_map/ppermute | solution.py:353
  21.9 8.4 %copy-start.11 = (f32[128]{0:T(128)S(1)}, f32[128]{0:T(128)}, u32[]{:S(2)}) copy-start(f32[128]{0:T(128)} %param.12) | copy-start | bytes 1540
  31.8 0.8 %copy-start.4 = (f32[256,512]{1,0:T(8,128)}, f32[256,512]{1,0:T(8,128)S(1)}, u32[]{:S(2)}) copy-start(f32[256,512]{1,0:T(8,128)S(1)} %get-tuple-element.15.base_ref) | copy-start | bytes 1572868
  43.3 8.7 %copy-start.5 = (f32[256,512]{1,0:T(8,128)S(1)}, f32[256,512]{1,0:T(8,128)}, u32[]{:S(2)}) copy-start(f32[256,512]{1,0:T(8,128)} %copy-done.4) | copy-start | bytes 1572868
